TPU v7x, 32 devices: a whole 2x2x4 slice. The times are simulated.
32 devices in a mesh: groups: 2 (over x), row: 16 (over z, y, core).
Axes of the slice: x: 2, y: 2, z: 4, core: 2. Of those that a mesh axis runs over, the one named last changes fastest.
Arguments:
- alignment_input: bfloat16 [64, 256, 64], P('groups', 'row'), parts along dimension 0, may hold values from -6 to 6
- alignment_mask: int32 [64, 256], P('groups'), parts along dimension 0, may hold values from 0 to 1, as said below
- residue_mask: int32 [512], P('groups'), parts along dimension 0, may hold values 0 or 1
- left_weight: bfloat16 [64, 32], replicated, may hold values from -0.75 to 0.75
- right_weight: bfloat16 [64, 32], replicated, may hold values from -0.75 to 0.75
- output_weight: bfloat16 [1024, 128], replicated, may hold values from -0.1875 to 0.1875
- pairwise_gradient: bfloat16 [512, 256, 128], P(('groups', 'row')), parts along dimension 0, may hold values from -6 to 6
Outputs:
- msa_grad: float32 [64, 256, 64], P('groups', 'row'), parts along dimension 0
There are 2 independent parts, one for each index of `groups`. A program takes and returns all parts, laid end to end along the dimension named above; an argument that names none is the same for every part. Nothing has to cross between parts.
Inputs may be any that keep to these rules, and one draw needn't show every extreme that they name: `alignment_mask`: sequence 0 is present at every residue.
All inputs are finite; a program needn't handle non-finite values.
Results may differ from a plain program's by a relative error of at most 0.005.
Values may be sent and summed in bfloat16 or wider, within the bound.
No kernel may reach another device: no remote copies, remote signals or barrier semaphores. Data moves between devices by JAX's collectives and lax.ppermute only.
A program may use at most 128 MiB of HBM per device.

v0:
```python
import jax
import jax.numpy as jnp
from jax import lax
from jax.sharding import PartitionSpec as P

HIDDEN_CHANNELS = 32


def layer_normalize(alignment_input):
    value_rows = alignment_input.astype(jnp.float32)
    centered = value_rows - jnp.mean(value_rows, axis=-1, keepdims=True)
    inverse_deviation = lax.rsqrt(jnp.mean(centered * centered, axis=-1, keepdims=True) + 1e-05)
    return (centered * inverse_deviation, inverse_deviation)


def project(normalized_input, weight, presence_mask):
    feature_depth, width, channels = normalized_input.shape
    normed_half = normalized_input.astype(jnp.bfloat16)
    flat = jnp.dot(
        normed_half.reshape(feature_depth * width, channels),
        weight,
        preferred_element_type=jnp.float32,
    )
    return (presence_mask[:, :, None] * flat.reshape(feature_depth, width, weight.shape[1])).astype(
        jnp.bfloat16
    )


def tile_grad(grad_tile, norm_tile, output_weight):
    first, second, width = grad_tile.shape
    flat = jnp.einsum(
        "pk,ck->pc",
        grad_tile.reshape(first * second, width),
        output_weight,
        preferred_element_type=jnp.float32,
    )
    scaled = (
        flat.reshape(first, second, HIDDEN_CHANNELS, HIDDEN_CHANNELS) / norm_tile[:, :, None, None]
    )
    return scaled.astype(jnp.bfloat16)


def shards(
    alignment_input,
    alignment_mask,
    residue_mask,
    left_weight,
    right_weight,
    output_weight,
    pairwise_gradient,
):
    feature_depth, local_rows, feature_block = alignment_input.shape
    hidden = left_weight.shape[1]
    begin = lax.axis_index("row") * local_rows
    normalized_input, inverse_deviation = layer_normalize(alignment_input)
    presence_mask_full = alignment_mask.astype(jnp.float32)
    presence_mask = lax.dynamic_slice_in_dim(presence_mask_full, begin, local_rows, 1)
    left = project(normalized_input, left_weight, presence_mask)
    right = project(normalized_input, right_weight, presence_mask)
    left_rows = jnp.transpose(left, (1, 0, 2))
    right_rows = jnp.transpose(right, (1, 0, 2))
    right_panel = right_rows.reshape(local_rows, feature_depth * hidden)
    counts = jnp.dot(presence_mask.T, presence_mask_full, precision=lax.Precision.HIGHEST) + 0.001
    residue = residue_mask.astype(jnp.bfloat16)
    res_own = lax.dynamic_slice_in_dim(residue, begin, local_rows, 0)
    masked_grad = pairwise_gradient * (res_own[:, None] * residue[None, :])[:, :, None]
    panel = lax.all_gather(right_panel, "row", axis=0, tiled=True)
    width = panel.shape[0]
    tiles = tile_grad(masked_grad, counts, output_weight)
    right_piece = panel.reshape(width, feature_depth, hidden)
    left_total = jnp.einsum("ijce,jse->isc", tiles, right_piece, preferred_element_type=jnp.float32)
    partial_sum = jnp.einsum("ijce,isc->jse", tiles, left_rows, preferred_element_type=jnp.float32)
    right_total = partial_sum.reshape(width, feature_depth * hidden)
    right_sum = lax.psum_scatter(right_total, "row", scatter_dimension=0, tiled=True).reshape(
        local_rows, feature_depth, hidden
    )
    left_grad = presence_mask[:, :, None] * jnp.transpose(left_total, (1, 0, 2))
    right_grad = presence_mask[:, :, None] * jnp.transpose(right_sum, (1, 0, 2))
    normed_grad = jnp.einsum(
        "snc,mc->snm", left_grad, left_weight.astype(jnp.float32), precision=lax.Precision.HIGHEST
    )
    normed_grad = normed_grad + jnp.einsum(
        "snc,mc->snm", right_grad, right_weight.astype(jnp.float32), precision=lax.Precision.HIGHEST
    )
    mean_grad = jnp.mean(normed_grad, axis=-1, keepdims=True)
    mean_cross = jnp.mean(normed_grad * normalized_input, axis=-1, keepdims=True)
    return inverse_deviation * (normed_grad - mean_grad - normalized_input * mean_cross)


def solution(mesh):
    return jax.shard_map(
        shards,
        mesh=mesh,
        in_specs=(
            P("groups", "row", None),
            P("groups", None),
            P("groups"),
            P(),
            P(),
            P(),
            P(("groups", "row"), None, None),
        ),
        out_specs=P("groups", "row", None),
        check_vma=False,
    )
```

profile of v0, /device:TPU:0, one launch (start us, length us, event | category | flops | bytes accessed | tf_op | source)
XLA Modules:
  0.0 100.0 jit_solution(11952852471276327522)
XLA Ops:
  6.5 0.8 convert_element_type.27
  7.3 0.1 constant_dynamic-slice_fusion
  7.5 0.7 convert_element_type.30
  8.2 0.1 dynamic_slice.7
  8.3 0.1 broadcast_multiply_fusion
  8.3 1.0 %convert_reduce_fusion = f32[32,16]{0,1:T(8,128)S(1)} fusion(bf16[32,16,64]{2,1,0:T(8,128)(2,1)} %param.7), kind=kLoop, calls=%fused_computation.23 | loop fusion | flops 65024 | bytes 67584 | tf_op jit(solution)/shard_map/reduce_sum | solution.py:11
  9.4 1.2 %fusion.31 = f32[32,16]{0,1:T(8,128)S(1)} fusion(f32[32,16]{0,1:T(8,128)S(1)} %broadcast_multiply_fusion.3, bf16[32,16,64]{2,1,0:T(8,128)(2,1)} %param.7), kind=kLoop, calls=%fused_computation.32 | loop fusion | flops 130560 | bytes 69632 | tf_op jit(solution)/shard_map/reduce_sum | solution.py:12
  10.6 1.0 convolution_add_fusion.1
  11.6 6.1 %divide_convert_fusion = bf16[16,256,32,32]{1,3,2,0:T(8,128)(2,1)} fusion(f32[16,256]{1,0:T(8,128)S(1)} %convolution_add_fusion.1, bf16[32,32,128,1]{2,1,0,3:T(8,128)(2,1)S(1)} %bitcast.68, bf16[16,256,128]{2,1,0:T(8,128)(2,1)} %param.13, bf16[16,256]{1,0:T(8,128)(2,1)S(1)} %broadcast_multiply_fusion), kind=kOutput, calls=%fused_computation | convolution fusion | flops 1084227584 | bytes 9723904 | tf_op jit(solution)/shard_map/pk,ck->pc/dot_general | solution.py:31
  17.8 10.0 %fusion.4 = f32[256,32,32]{0,1,2:T(8,128)S(1)} fusion(bf16[16,256,32,32]{1,3,2,0:T(8,128)(2,1)} %divide_convert_fusion, f32[16,32]{1,0:T(8,128)S(1)} %copy.23, f32[32,16]{0,1:T(8,128)S(1)} %add_rsqrt_fusion, f32[32,16]{0,1:T(8,128)S(1)} %broadcast_multiply_fusion.3, bf16[32,16,64]{2,1,0:T(8,128)(2,1)S(1)} %copy-done.1, bf16[64,32]{0,1:T(8,128)(2,1)S(1)} %copy-done.2), kind=kOutput, calls=%fused_computation.5 | convolution fusion | flops 270696448 | bytes 9512960 | tf_op jit(solution)/shard_map/ijce,isc->jse/dot_general | solution.py:72
  27.8 0.6 copy.28
  28.4 1.4 %copy.35 = f32[256,1024]{1,0:T(8,128)} copy(f32[256,1024]{0,1:T(8,128)S(1)} %bitcast.69) | data formatting | bytes 2097152
  29.9 0.3 fusion.15
  30.3 0.2 reshape.74
  30.4 24.8 %all_gather.3 = bf16[256,1024]{1,0:T(8,128)(2,1)S(1)} all-gather(bf16[16,1024]{1,0:T(8,128)(2,1)S(1)} %reshape.74), channel_id=1, replica_groups=mesh['groups'=2,'row'=16] {'row'}, dimensions={0}, use_global_device_ids=true | all-gather | bytes 557056 | tf_op jit(solution)/shard_map/all_gather | solution.py:67
  55.2 0.2 copy.24
  55.4 13.7 %fusion.12 = f32[32,16,32]{2,0,1:T(8,128)S(1)} fusion(bf16[16,256,32,32]{1,3,2,0:T(8,128)(2,1)} %divide_convert_fusion, bf16[256,32,32]{0,2,1:T(8,128)(2,1)S(1)} %bitcast.71, f32[32,16]{0,1:T(8,128)S(1)} %copy.22), kind=kOutput, calls=%fused_computation.12 | convolution fusion | flops 268451840 | bytes 8980480 | tf_op jit(solution)/shard_map/ijce,jse->isc/dot_general | solution.py:71
  69.1 0.2 fusion.42
  69.4 20.7 %reduce-scatter.4.cloned.1.call-done = f32[16,1024]{1,0:T(8,128)} async-done(((f32[256,1024]{1,0:T(8,128)}), f32[16,1024]{1,0:T(8,128)}) %reduce-scatter.4.cloned.1.call-update) | async-done | bytes 65552
  90.1 1.0 %copy.36 = f32[16,1024]{0,1:T(8,128)S(1)} copy(f32[16,1024]{1,0:T(8,128)} %reduce-scatter.4.cloned.1.call-done) | data formatting | bytes 131072
  91.2 0.3 copy.34
  91.4 0.5 fusion.47
  91.9 0.3 fusion.30
  92.3 0.9 copy.30
  (16 shorter events, 0.3 us)
Async XLA Ops:
  6.5 5.1 %copy-start = (bf16[1024,128]{1,0:T(8,128)(2,1)S(1)}, bf16[1024,128]{1,0:T(8,128)(2,1)}, u32[]{:S(2)}) copy-start(bf16[1024,128]{1,0:T(8,128)(2,1)} %param.12) | copy-start | bytes 786436
  6.5 83.6 %reduce-scatter.4.cloned.1.call-start = ((), (), s32[]{:S(2)}) async-start(), calls=%async_computation.1 | async-start | bytes 1114112
  11.6 6.1 %copy-start.1 = (bf16[32,16,64]{2,1,0:T(8,128)(2,1)S(1)}, bf16[32,16,64]{2,1,0:T(8,128)(2,1)}, u32[]{:S(2)}) copy-start(bf16[32,16,64]{2,1,0:T(8,128)(2,1)} %param.7) | copy-start | bytes 196612
  11.6 6.1 %copy-start.2 = (bf16[64,32]{0,1:T(8,128)(2,1)S(1)}, bf16[64,32]{0,1:T(8,128)(2,1)}, u32[]{:S(2)}) copy-start(bf16[64,32]{0,1:T(8,128)(2,1)} %param.10) | copy-start | bytes 12292
  17.8 12.2 %copy-start.3 = (bf16[64,32]{0,1:T(8,128)(2,1)S(1)}, bf16[64,32]{0,1:T(8,128)(2,1)}, u32[]{:S(2)}) copy-start(bf16[64,32]{0,1:T(8,128)(2,1)} %param.11) | copy-start | bytes 12292
Sparse Core Ops, SparseCore 0:
  30.0 60.1 reduce-scatter.3
where the time goes:
time: 100 us
  matrix products  31.9 us (32%)
  blocking collectives  24.8 us (25%)
  waiting for transfers between devices  20.8 us (21%)
  between operations  13.5 us (14%)
  local copies, waits for them, and re-layouts  4.93 us (5%)
  other arithmetic  4.13 us (4%)
    all_gather x1, blocking collectives, shards(): panel = lax.all_gather(right_panel, 'row', axis=0, tiled=True)  24.8 us
    unnamed x2, waiting for transfers between devices  20.8 us
    dot_general x1, matrix products, shards(): jnp.einsum('ijce,jse->isc', tiles, right_piece, preferred_element_type=jn...  13.7 us
    dot_general x1, matrix products, shards(): jnp.einsum('ijce,isc->jse', tiles, left_rows, preferred_element_type=jnp....  10 us
    dot_general x1, matrix products, tile_grad(): jnp.einsum('pk,ck->pc', grad_tile.reshape(first * second, width), output_...  6.11 us
    unnamed x10, local copies, waits for them, and re-layouts  2.46 us
  transfers between devices with their start and end apart: 1, of which 1 were waited for; matrix products, arithmetic and copies ran while one was open for 15% of the time, Pallas kernels for 0%

commit v1 on v0

v1 whole, which is shorter than its diff:
```python
import functools

import jax
import jax.numpy as jnp
from jax import lax
from jax.experimental import pallas as pl
from jax.experimental.pallas import tpu as pltpu
from jax.sharding import PartitionSpec as P

F32 = jnp.float32
BF16 = jnp.bfloat16
NT = (((1,), (1,)), ((), ()))
PARAMS = pltpu.CompilerParams(vmem_limit_bytes=56 * 1024 * 1024)


def iota(shape, axis):
    return lax.broadcasted_iota(jnp.int32, shape, axis)


def own_presence(mask, me, rows):
    pick = iota((mask.shape[1], rows), 0) == me * rows + iota((mask.shape[1], rows), 1)
    return jnp.dot(mask.astype(F32).astype(BF16), pick.astype(F32).astype(BF16), preferred_element_type=F32)


def presence_row(own, sequence_major):
    depth, rows = own.shape
    count = depth * rows
    column = iota((rows, count), 1)
    residue = column % rows if sequence_major else column // depth
    spread = (residue == iota((rows, count), 0)).astype(F32).astype(BF16)
    wide = jnp.dot(own.astype(BF16), spread, preferred_element_type=F32)
    column = iota((depth, count), 1)
    sequence = column // rows if sequence_major else column % depth
    return jnp.sum(jnp.where(sequence == iota((depth, count), 0), wide, 0.0), axis=0, keepdims=True)


def project_kernel(rows, x_ref, mask_ref, lw_ref, rw_ref, left_ref, right_ref, normed, flat):
    count, channels = x_ref.shape
    depth = count // rows
    hidden = lw_ref.shape[1]
    me = lax.axis_index("row")
    value = x_ref[...].astype(F32)
    centered = value - jnp.mean(value, axis=-1, keepdims=True)
    recip = lax.rsqrt(jnp.mean(centered * centered, axis=-1, keepdims=True) + 1e-05)
    value = centered * recip
    normed[...] = value
    own = own_presence(mask_ref[...], me, rows)
    rwt = rw_ref[...].astype(F32).T.astype(BF16)
    right = lax.dot_general(rwt, value.astype(BF16), NT, preferred_element_type=F32)
    right = right * presence_row(own, True)
    for s in range(depth):
        flat[pl.ds(s, hidden, stride=depth), :] = right[:, s * rows : (s + 1) * rows]
    right_ref[...] = flat[...].T.astype(BF16)
    by_residue = jnp.concatenate(
        [normed[pl.ds(i, depth, stride=rows), :] for i in range(rows)], axis=0
    ).astype(BF16)
    lwt = lw_ref[...].astype(F32).T.astype(BF16)
    left = lax.dot_general(lwt, by_residue, NT, preferred_element_type=F32)
    left_ref[...] = (left * presence_row(own, False)).astype(BF16)


def partial_kernel(
    rows, size, g_ref, mask_ref, res_ref, left_ref, ow_ref,
    keep_ref, send_ref, scaled_ref, owp_ref,
    inverse, ow_wide, stack, spread,
):
    depth, width = mask_ref.shape
    hidden = left_ref.shape[0]
    pair = g_ref.shape[2]
    me = lax.axis_index("row")
    bits = size.bit_length() - 1
    fold = 256 // hidden
    groups = hidden // fold
    mask = mask_ref[...].astype(F32)
    own = own_presence(mask_ref[...], me, rows)
    residue = res_ref[...].astype(F32)
    residue_own = own_presence(jnp.broadcast_to(res_ref[...], (8, width)), me, rows)[:1]
    tall = jnp.concatenate([mask, jnp.broadcast_to(residue, (8, width))], axis=0).T
    counts = jnp.dot(tall[:, :depth].astype(BF16), own.astype(BF16), preferred_element_type=F32) + 0.001
    inverse[...] = tall[:, depth : depth + 1] * residue_own / counts

    def scale(p, _):
        relative = 0
        for t in range(bits):
            relative = relative + (((p >> (bits - 1 - t)) & 1) << t)
        begin = pl.multiple_of((me ^ relative) * rows, rows)
        factor = inverse[pl.ds(begin, rows), :]
        for i in range(rows):
            block = g_ref[i, pl.ds(begin, rows), :].astype(F32) * factor[:, i : i + 1]
            scaled_ref[pl.ds(pl.multiple_of(p * rows, rows), rows), i * pair : (i + 1) * pair] = block.astype(BF16)
        return 0

    lax.fori_loop(0, size, scale, 0)
    ow_wide[...] = ow_ref[...].astype(F32)
    for e in range(hidden):
        owp_ref[e * hidden : (e + 1) * hidden, :] = ow_wide[pl.ds(e, hidden, stride=hidden), :].astype(BF16)
    for g in range(groups):
        stack[g * pair : (g + 1) * pair, :] = owp_ref[g * 256 : (g + 1) * 256, :].T
    per = 128 // depth
    blocks = rows // per
    tile = jnp.concatenate([left_ref[:, g * 128 : (g + 1) * 128] for g in range(blocks)], axis=0)
    column = iota((128, per * 256), 1)
    repeat = (column % depth + depth * (column // 256)) == iota((128, per * 256), 0)
    wide = jnp.dot(tile, repeat.astype(F32).astype(BF16), preferred_element_type=F32)
    diagonal = iota((256, 256), 0) // hidden == iota((256, 256), 1) // depth
    for i in range(rows):
        g, q = divmod(i, per)
        own_left = wide[g * hidden : (g + 1) * hidden, q * 256 : (q + 1) * 256]
        block = jnp.where(diagonal, jnp.concatenate([own_left] * fold, axis=0), 0.0).astype(BF16)
        out = jnp.dot(stack[...], block, preferred_element_type=F32).astype(BF16)
        for g in range(groups):
            spread[i * pair : (i + 1) * pair, g * 256 : (g + 1) * 256] = out[g * pair : (g + 1) * pair, :]
    half = width // 2
    send_ref[...] = jnp.dot(scaled_ref[half:, :], spread[...], preferred_element_type=F32).astype(BF16)
    keep_ref[...] = jnp.dot(scaled_ref[:half, :], spread[...], preferred_element_type=F32)


def left_kernel(
    rows, *refs,
):
    (*pieces, scaled_ref, owp_ref, x_ref, mask_ref, lw_ref, grad_ref, normed_ref, recip_ref, presence_ref,
     panel, outer, total) = refs
    count, channels = x_ref.shape
    depth = count // rows
    pair = owp_ref.shape[1]
    hidden = lw_ref.shape[1]
    me = lax.axis_index("row")
    begin = 0
    for piece in pieces:
        panel[begin : begin + piece.shape[0], :] = piece[...]
        begin += piece.shape[0]
    turned = panel[...].T
    for q in range(rows // 2):
        out = jnp.dot(turned, scaled_ref[:, q * 2 * pair : (q + 1) * 2 * pair], preferred_element_type=F32).astype(BF16)
        for h in range(2):
            i = 2 * q + h
            outer[:, i * depth : (i + 1) * depth, :] = out[:, h * pair : (h + 1) * pair].reshape(hidden, depth, pair)
    acc = jnp.zeros((count, hidden), F32)
    for e in range(0, hidden, 2):
        lhs = jnp.concatenate([outer[e], outer[e + 1]], axis=1)
        rhs = jnp.concatenate([owp_ref[e * hidden : (e + 1) * hidden, :], owp_ref[(e + 1) * hidden : (e + 2) * hidden, :]], axis=1)
        acc = acc + lax.dot_general(lhs, rhs, NT, preferred_element_type=F32)
    total[...] = acc
    by_sequence = jnp.concatenate([total[pl.ds(s, rows, stride=depth), :] for s in range(depth)], axis=0)
    grad_ref[...] = lax.dot_general(
        lw_ref[...].astype(F32), by_sequence, NT, preferred_element_type=F32, precision=lax.Precision.HIGHEST
    )
    value = x_ref[...].astype(F32).T
    centered = value - jnp.mean(value, axis=0, keepdims=True)
    recip = lax.rsqrt(jnp.mean(centered * centered, axis=0, keepdims=True) + 1e-05)
    normed_ref[...] = centered * recip
    recip_ref[...] = recip
    presence_ref[...] = presence_row(own_presence(mask_ref[...], me, rows), True)


def final_kernel(rows, keep_ref, got_ref, rw_ref, grad_ref, normed_ref, recip_ref, presence_ref, out_ref, flat, lanes):
    hidden = rw_ref.shape[1]
    depth = keep_ref.shape[1] // hidden
    flat[...] = (keep_ref[...] + got_ref[...].astype(F32)).T
    for s in range(depth):
        lanes[:, s * rows : (s + 1) * rows] = flat[pl.ds(s, hidden, stride=depth), :]
    grad = jnp.dot(rw_ref[...].astype(F32), lanes[...], preferred_element_type=F32, precision=lax.Precision.HIGHEST)
    grad = (grad + grad_ref[...]) * presence_ref[...]
    normed = normed_ref[...]
    mean = jnp.mean(grad, axis=0, keepdims=True)
    cross = jnp.mean(grad * normed, axis=0, keepdims=True)
    out_ref[...] = (recip_ref[...] * (grad - mean - normed * cross)).T


def shape(dims, dtype):
    return jax.ShapeDtypeStruct(dims, dtype)


def shards(size, x, mask, residue_mask, lw, rw, ow, g):
    depth, rows, channels = x.shape
    hidden = lw.shape[1]
    width, pair = g.shape[1:]
    flat_width = depth * hidden
    x = x.reshape(depth * rows, channels)
    residue = residue_mask.reshape(1, width)
    vmem = pl.BlockSpec(memory_space=pltpu.VMEM)

    def exchange(value, bit):
        return lax.ppermute(value, "row", [(d, d ^ bit) for d in range(size)])

    left, right = pl.pallas_call(
        functools.partial(project_kernel, rows),
        out_shape=(shape((hidden, depth * rows), BF16), shape((rows, flat_width), BF16)),
        in_specs=[vmem] * 4,
        out_specs=(vmem, vmem),
        scratch_shapes=[pltpu.VMEM((depth * rows, channels), F32), pltpu.VMEM((flat_width, rows), F32)],
        compiler_params=PARAMS,
        name="project",
    )(x, mask, lw, rw)
    keep, send, scaled, owp = pl.pallas_call(
        functools.partial(partial_kernel, rows, size),
        out_shape=(
            shape((width // 2, flat_width), F32),
            shape((width // 2, flat_width), BF16),
            shape((width, rows * pair), BF16),
            shape(ow.shape, BF16),
        ),
        in_specs=[vmem] * 5,
        out_specs=(vmem,) * 4,
        scratch_shapes=[
            pltpu.VMEM((width, rows), F32),
            pltpu.VMEM(ow.shape, F32),
            pltpu.VMEM((ow.shape[0] // 256 * pair, 256), BF16),
            pltpu.VMEM((rows * pair, flat_width), BF16),
        ],
        compiler_params=PARAMS,
        cost_estimate=pl.CostEstimate(flops=4 * 2**30, bytes_accessed=4 << 20, transcendentals=0),
        name="partial",
    )(g, mask, residue, left, ow)
    pieces = [right]
    bit = size // 2
    while bit:
        block = pieces[0] if len(pieces) == 1 else jnp.concatenate(pieces, axis=0)
        pieces.append(exchange(block, bit))
        bit //= 2
    bit = 1
    got = exchange(send, bit)
    while keep.shape[0] > rows:
        total = keep + got.astype(F32)
        half = total.shape[0] // 2
        bit *= 2
        keep = total[:half]
        got = exchange(total[half:].astype(BF16), bit)
    grad, normed, recip, presence = pl.pallas_call(
        functools.partial(left_kernel, rows),
        out_shape=(
            shape((channels, depth * rows), F32),
            shape((channels, depth * rows), F32),
            shape((1, depth * rows), F32),
            shape((1, depth * rows), F32),
        ),
        in_specs=[vmem] * (len(pieces) + 5),
        out_specs=(vmem,) * 4,
        scratch_shapes=[
            pltpu.VMEM((width, flat_width), BF16),
            pltpu.VMEM((hidden, depth * rows, pair), BF16),
            pltpu.VMEM((depth * rows, hidden), F32),
        ],
        compiler_params=PARAMS,
        cost_estimate=pl.CostEstimate(flops=4 * 2**30, bytes_accessed=4 << 20, transcendentals=0),
        name="left",
    )(*pieces, scaled, owp, x, mask, lw)
    out = pl.pallas_call(
        functools.partial(final_kernel, rows),
        out_shape=shape((depth * rows, channels), F32),
        in_specs=[vmem] * 7,
        out_specs=vmem,
        scratch_shapes=[pltpu.VMEM((flat_width, rows), F32), pltpu.VMEM((hidden, depth * rows), F32)],
        compiler_params=PARAMS,
        name="final",
    )(keep, got, rw, grad, normed, recip, presence)
    return out.reshape(depth, rows, channels)


def solution(mesh):
    return jax.shard_map(
        functools.partial(shards, mesh.shape["row"]),
        mesh=mesh,
        in_specs=(
            P("groups", "row", None),
            P("groups", None),
            P("groups"),
            P(),
            P(),
            P(),
            P(("groups", "row"), None, None),
        ),
        out_specs=P("groups", "row", None),
        check_vma=False,
    )
```

time: 100 us -> 46.6 us (0.47)
  matrix products: 31.9 us -> 0 us
  blocking collectives: 24.8 us -> 0 us
  Pallas kernels: 0 us -> 19.3 us
  starting transfers between devices: 0.01 us -> 13.5 us
  between operations: 13.5 us -> 0.07 us
  waiting for transfers between devices: 20.8 us -> 7.64 us
  other arithmetic: 4.13 us -> 1.18 us
    dot_general x7 -> x0, matrix products: 31.9 us -> none  [the longest x1 13.7 us: shards(): jnp.einsum('ijce,jse->isc', tiles, right_piece, preferred_element_type=jn...]
    all_gather x1 -> x0, blocking collectives: 24.8 us -> none  [shards(): panel = lax.all_gather(right_panel, 'row', axis=0, tiled=True)]
    unnamed x2 -> x0, waiting for transfers between devices: 20.8 us -> none
    pallas_call x0 -> x4, Pallas kernels: none -> 19.3 us  [the longest x1 7.16 us: shards(): pl.pallas_call(functools.partial(partial_kernel, rows, size), out_shape=(...]
    ppermute x0 -> x8, starting transfers between devices: none -> 13.5 us  [exchange(): return lax.ppermute(value, 'row', [(d, d ^ bit) for d in range(size)])]
    ppermute x0 -> x8, waiting for transfers between devices: none -> 7.64 us  [exchange(): return lax.ppermute(value, 'row', [(d, d ^ bit) for d in range(size)])]
    reduce_sum x2 -> x0, other arithmetic: 2.21 us -> none  [the longest x1 1.16 us: layer_normalize(): jnp.mean(centered * centered, axis=-1, keepdims=True) + 1e-05]
    unnamed x10 -> x16, local copies, waits for them, and re-layouts: 2.46 us -> 4.01 us
  transfers between devices with their start and end apart: 1 -> 8, of which waited for: 1 -> 4; matrix products, arithmetic and copies ran while one was open for 15% -> 4% of each run, Pallas kernels for 0% -> 15%
where the time goes in v1:
time: 46.6 us; the launch traced here: 46.3 us
  Pallas kernels  19.3 us (41%)
  starting transfers between devices  13.5 us (29%)
  waiting for transfers between devices  7.64 us (16%)
  local copies, waits for them, and re-layouts  4.67 us (10%)
  other arithmetic  1.18 us (3%)
    ppermute x8, starting transfers between devices, exchange(): return lax.ppermute(value, 'row', [(d, d ^ bit) for d in range(size)])  13.5 us
    ppermute x8, waiting for transfers between devices, exchange(): return lax.ppermute(value, 'row', [(d, d ^ bit) for d in range(size)])  7.64 us
    pallas_call x1, Pallas kernels, shards(): pl.pallas_call(functools.partial(partial_kernel, rows, size), out_shape=(...  7.16 us
    pallas_call x1, Pallas kernels, shards(): pl.pallas_call(functools.partial(left_kernel, rows), out_shape=(shape((ch...  6.98 us
    unnamed x16, local copies, waits for them, and re-layouts  4.01 us
    pallas_call x1, Pallas kernels, shards(): pl.pallas_call(functools.partial(final_kernel, rows), out_shape=shape((de...  2.67 us
    pallas_call x1, Pallas kernels, shards(): pl.pallas_call(functools.partial(project_kernel, rows), out_shape=(shape(...  2.47 us
    add x3, other arithmetic, shards(): total = keep + got.astype(F32)  1.15 us
  transfers between devices with their start and end apart: 8, of which 4 were waited for; matrix products, arithmetic and copies ran while one was open for 4% of the time, Pallas kernels for 15%

profile of v1, /device:TPU:0, one launch (start us, length us, event | category | flops | bytes accessed | tf_op | source)
XLA Modules:
  0.0 46.3 jit_solution(11512591515328082094)
XLA Ops:
  0.0 1.4 %copy.8.lw_ref.refs_9_ = bf16[64,32]{1,0:T(8,128)(2,1)} copy(bf16[64,32]{0,1:T(8,128)(2,1)} %param.10) | data formatting | bytes 8192 | tf_op args[3]
  1.4 0.7 %copy.9.rw_ref = bf16[64,32]{1,0:T(8,128)(2,1)} copy(bf16[64,32]{0,1:T(8,128)(2,1)S(1)} %copy-done.5) | data formatting | bytes 8192 | tf_op args[4]
  2.1 2.5 %project.1 = (bf16[32,512]{1,0:T(8,128)(2,1)}, bf16[16,1024]{1,0:T(8,128)(2,1)}) custom-call(bf16[512,64]{1,0:T(8,128)(2,1)} %bitcast.3, s32[32,256]{1,0:T(8,128)} %refs_8_.1, bf16[64,32]{1,0:T(8,128)(2,1)} %copy.8.lw_ref.refs_9_, bf16[64,32]{1,0:T(8,128)(2,1)} %copy.9.rw_ref), custom_call_target="tpu_custom_call" | custom-call | tf_op jit(solution)/shard_map/project/pallas_call | solution.py:186
  4.6 7.2 %partial.1 = (f32[128,1024]{1,0:T(8,128)}, bf16[128,1024]{1,0:T(8,128)(2,1)}, bf16[256,2048]{1,0:T(8,128)(2,1)}, bf16[1024,128]{1,0:T(8,128)(2,1)}) custom-call(bf16[16,256,128]{2,1,0:T(8,128)(2,1)} %g_ref.1, s32[32,256]{1,0:T(8,128)} %refs_8_.1, s32[1,256]{1,0:T(1,128)} %bitcast.5, bf16[32,512]{1,0:T(8,128)(2,1)} %get-tuple-element.15.left_ref, ...), custom_call_target="tpu_custom_call" | custom-call | flops 4294967296 | bytes 4194304 | tf_op jit(solution)/shard_map/partial/pallas_call | solution.py:195
  11.7 0.5 collective-permute-start
  12.2 3.7 %collective-permute-start.4 = (bf16[16,1024]{1,0:T(8,128)(2,1)S(1)}, bf16[16,1024]{1,0:T(8,128)(2,1)S(1)}, u32[]{:S(2)}, u32[]{:S(2)}) collective-permute-start(bf16[16,1024]{1,0:T(8,128)(2,1)S(1)} %copy-done), channel_id=1, source_target_pairs={{0,8},{1,9},{2,10},{3,11},{4,12},{5,13},{6,14},{7,15},{8,0},{9,1},... | collective-permute-start | bytes 98312 | tf_op jit(solution)/shard_map/ppermute | solution.py:184
  15.8 2.0 %collective-permute-done.4.refs_1_ = bf16[16,1024]{1,0:T(8,128)(2,1)S(1)} collective-permute-done((bf16[16,1024]{1,0:T(8,128)(2,1)S(1)}, bf16[16,1024]{1,0:T(8,128)(2,1)S(1)}, u32[]{:S(2)}, u32[]{:S(2)}) %collective-permute-start.4) | collective-permute-done | bytes 32800 | tf_op jit(solution)/shard_map/ppermute | solution.py:184
  17.8 1.9 %collective-permute-start.5 = (bf16[32,1024]{1,0:T(8,128)(2,1)S(1)}, bf16[32,1024]{1,0:T(8,128)(2,1)S(1)}, u32[]{:S(2)}, u32[]{:S(2)}) collective-permute-start(bf16[32,1024]{1,0:T(8,128)(2,1)S(1)} %pad_maximum_fusion.2), channel_id=1, source_target_pairs={{0,4},{1,5},{2,6},{3,7},{4,0},{5,1},{6,2},{7,3},{8,12},{9,13},{10,... | collective-permute-start | bytes 196616 | tf_op jit(solution)/shard_map/ppermute | solution.py:184
  19.7 1.1 %convert_add_fusion = f32[128,1024]{1,0:T(8,128)S(1)} fusion(f32[128,1024]{1,0:T(8,128)} %get-tuple-element.16, bf16[128,1024]{1,0:T(8,128)(2,1)S(1)} %collective-permute-done), kind=kLoop, calls=%fused_computation | loop fusion | flops 262144 | bytes 1310720 | tf_op jit(solution)/shard_map/add | solution.py:224
  20.8 1.6 %collective-permute-start.1 = (bf16[64,1024]{1,0:T(8,128)(2,1)S(1)}, bf16[64,1024]{1,0:T(8,128)(2,1)S(1)}, u32[]{:S(2)}, u32[]{:S(2)}) collective-permute-start(bf16[64,1024]{1,0:T(8,128)(2,1)S(1)} %slice.38), channel_id=1, source_target_pairs={{0,2},{1,3},{2,0},{3,1},{4,6},{5,7},{6,4},{7,5},{8,10},{9,11},{10,... | collective-permute-start | bytes 393224 | tf_op jit(solution)/shard_map/ppermute | solution.py:184
  22.5 1.5 %collective-permute-start.6 = (bf16[64,1024]{1,0:T(8,128)(2,1)S(1)}, bf16[64,1024]{1,0:T(8,128)(2,1)S(1)}, u32[]{:S(2)}, u32[]{:S(2)}) collective-permute-start(bf16[64,1024]{1,0:T(8,128)(2,1)S(1)} %pad_maximum_fusion.1), channel_id=1, source_target_pairs={{0,2},{1,3},{2,0},{3,1},{4,6},{5,7},{6,4},{7,5},{8,10},{9,11},{10,... | collective-permute-start | bytes 393224 | tf_op jit(solution)/shard_map/ppermute | solution.py:184
  24.0 2.7 %collective-permute-done.1 = bf16[64,1024]{1,0:T(8,128)(2,1)S(1)} collective-permute-done((bf16[64,1024]{1,0:T(8,128)(2,1)S(1)}, bf16[64,1024]{1,0:T(8,128)(2,1)S(1)}, u32[]{:S(2)}, u32[]{:S(2)}) %collective-permute-start.1) | collective-permute-done | bytes 131104 | tf_op jit(solution)/shard_map/ppermute | solution.py:184
  26.8 0.8 %collective-permute-start.2 = (bf16[32,1024]{1,0:T(8,128)(2,1)S(1)}, bf16[32,1024]{1,0:T(8,128)(2,1)S(1)}, u32[]{:S(2)}, u32[]{:S(2)}) collective-permute-start(bf16[32,1024]{1,0:T(8,128)(2,1)S(1)} %slice.39), channel_id=1, source_target_pairs={{0,4},{1,5},{2,6},{3,7},{4,0},{5,1},{6,2},{7,3},{8,12},{9,13},{10,... | collective-permute-start | bytes 196616 | tf_op jit(solution)/shard_map/ppermute | solution.py:184
  27.5 0.6 %collective-permute-done.6.refs_3_ = bf16[64,1024]{1,0:T(8,128)(2,1)S(1)} collective-permute-done((bf16[64,1024]{1,0:T(8,128)(2,1)S(1)}, bf16[64,1024]{1,0:T(8,128)(2,1)S(1)}, u32[]{:S(2)}, u32[]{:S(2)}) %collective-permute-start.6) | collective-permute-done | bytes 131104 | tf_op jit(solution)/shard_map/ppermute | solution.py:184
  28.2 0.6 %copy-done.3 = bf16[64,1024]{1,0:T(8,128)(2,1)} copy-done((bf16[64,1024]{1,0:T(8,128)(2,1)}, bf16[64,1024]{1,0:T(8,128)(2,1)S(1)}, u32[]{:S(2)}) %copy-start.3) | copy-done | bytes 131096
  28.8 2.3 %collective-permute-done.2 = bf16[32,1024]{1,0:T(8,128)(2,1)S(1)} collective-permute-done((bf16[32,1024]{1,0:T(8,128)(2,1)S(1)}, bf16[32,1024]{1,0:T(8,128)(2,1)S(1)}, u32[]{:S(2)}, u32[]{:S(2)}) %collective-permute-start.2) | collective-permute-done | bytes 65568 | tf_op jit(solution)/shard_map/ppermute | solution.py:184
  31.1 0.6 %slice.31.keep_ref = f32[16,1024]{1,0:T(8,128)} slice(f32[32,1024]{1,0:T(8,128)S(1)} %slice_add_fusion.1), slice={[0:16], [0:1024]} | slice | bytes 131072 | tf_op jit(solution)/shard_map/slice | solution.py:227
  31.8 3.6 %collective-permute-start.3 = (bf16[16,1024]{1,0:T(8,128)(2,1)S(1)}, bf16[16,1024]{1,0:T(8,128)(2,1)S(1)}, u32[]{:S(2)}, u32[]{:S(2)}) collective-permute-start(bf16[16,1024]{1,0:T(8,128)(2,1)S(1)} %slice.40), channel_id=1, source_target_pairs={{0,8},{1,9},{2,10},{3,11},{4,12},{5,13},{6,14},{7,15},{8,0},{9,1},... | collective-permute-start | bytes 98312 | tf_op jit(solution)/shard_map/ppermute | solution.py:184
  35.4 0.0 collective-permute-done.7.refs_4_
  35.4 0.7 %copy-done.6 = bf16[128,1024]{1,0:T(8,128)(2,1)} copy-done((bf16[128,1024]{1,0:T(8,128)(2,1)}, bf16[128,1024]{1,0:T(8,128)(2,1)S(1)}, u32[]{:S(2)}) %copy-start.6) | copy-done | bytes 262168
  36.1 7.0 %left.1 = (f32[64,512]{1,0:T(8,128)}, f32[64,512]{1,0:T(8,128)}, f32[1,512]{1,0:T(1,128)}, f32[1,512]{1,0:T(1,128)}) custom-call(bf16[16,1024]{1,0:T(8,128)(2,1)} %get-tuple-element.18.refs_0_, bf16[16,1024]{1,0:T(8,128)(2,1)} %copy-done.1, bf16[32,1024]{1,0:T(8,128)(2,1)} %copy-done.2, bf16[64,1024]{1,0:T(8,128)(2,1)} %copy-done.3, ...), custom_call_target="tpu_custom_call" | custom-call | flops 4294967296 | bytes 4194304 | tf_op jit(solution)/shard_map/left/pallas_call | solution.py:229
  43.0 0.0 collective-permute-done.3.got_ref
  43.1 0.6 %copy-done.4 = bf16[16,1024]{1,0:T(8,128)(2,1)} copy-done((bf16[16,1024]{1,0:T(8,128)(2,1)}, bf16[16,1024]{1,0:T(8,128)(2,1)S(1)}, u32[]{:S(2)}) %copy-start.4) | copy-done | bytes 32792
  43.6 2.7 %final.1 = f32[512,64]{1,0:T(8,128)} custom-call(f32[16,1024]{1,0:T(8,128)} %slice.31.keep_ref, bf16[16,1024]{1,0:T(8,128)(2,1)} %copy-done.4, bf16[64,32]{1,0:T(8,128)(2,1)} %copy.9.rw_ref, f32[64,512]{1,0:T(8,128)} %get-tuple-element.21.grad_ref, f32[64,512]{1,0:T(8,128)} %get-tuple-element.22.normed_ref, f32[1,512]{1,0:T(1,128)} %get-tuple-element.23.recip_ref, ...), custom_call_target="tpu_custom_call" | custom-call | tf_op jit(solution)/shard_map/final/pallas_call | solution.py:248
  (22 shorter events, 0.1 us)
Async XLA Ops:
  0.0 1.4 %copy-start.5 = (bf16[64,32]{0,1:T(8,128)(2,1)S(1)}, bf16[64,32]{0,1:T(8,128)(2,1)}, u32[]{:S(2)}) copy-start(bf16[64,32]{0,1:T(8,128)(2,1)} %param.11) | copy-start | bytes 12292
  4.6 7.6 %copy-start = (bf16[16,1024]{1,0:T(8,128)(2,1)S(1)}, bf16[16,1024]{1,0:T(8,128)(2,1)}, u32[]{:S(2)}) copy-start(bf16[16,1024]{1,0:T(8,128)(2,1)} %get-tuple-element.18.refs_0_) | copy-start | bytes 98308
  11.7 8.0 %collective-permute-start = (bf16[128,1024]{1,0:T(8,128)(2,1)}, bf16[128,1024]{1,0:T(8,128)(2,1)S(1)}, u32[]{:S(2)}, u32[]{:S(2)}) collective-permute-start(bf16[128,1024]{1,0:T(8,128)(2,1)} %get-tuple-element.17), channel_id=1, source_target_pairs={{0,1},{1,0},{2,3},{3,2},{4,5},{5,4},{6,7},{7,6},{8,9},{9,8},{10,11... | collective-permute-start | bytes 786440 | tf_op jit(solution)/shard_map/ppermute | solution.py:184
  12.2 5.7 %collective-permute-start.4 = (bf16[16,1024]{1,0:T(8,128)(2,1)S(1)}, bf16[16,1024]{1,0:T(8,128)(2,1)S(1)}, u32[]{:S(2)}, u32[]{:S(2)}) collective-permute-start(bf16[16,1024]{1,0:T(8,128)(2,1)S(1)} %copy-done), channel_id=1, source_target_pairs={{0,8},{1,9},{2,10},{3,11},{4,12},{5,13},{6,14},{7,15},{8,0},{9,1},... | collective-permute-start | bytes 98312 | tf_op jit(solution)/shard_map/ppermute | solution.py:184
  17.8 10.3 %copy-start.1 = (bf16[16,1024]{1,0:T(8,128)(2,1)}, bf16[16,1024]{1,0:T(8,128)(2,1)S(1)}, u32[]{:S(2)}) copy-start(bf16[16,1024]{1,0:T(8,128)(2,1)S(1)} %collective-permute-done.4.refs_1_) | copy-start | bytes 98308
  17.8 4.6 %collective-permute-start.5 = (bf16[32,1024]{1,0:T(8,128)(2,1)S(1)}, bf16[32,1024]{1,0:T(8,128)(2,1)S(1)}, u32[]{:S(2)}, u32[]{:S(2)}) collective-permute-start(bf16[32,1024]{1,0:T(8,128)(2,1)S(1)} %pad_maximum_fusion.2), channel_id=1, source_target_pairs={{0,4},{1,5},{2,6},{3,7},{4,0},{5,1},{6,2},{7,3},{8,12},{9,13},{10,... | collective-permute-start | bytes 196616 | tf_op jit(solution)/shard_map/ppermute | solution.py:184
  20.8 5.9 %collective-permute-start.1 = (bf16[64,1024]{1,0:T(8,128)(2,1)S(1)}, bf16[64,1024]{1,0:T(8,128)(2,1)S(1)}, u32[]{:S(2)}, u32[]{:S(2)}) collective-permute-start(bf16[64,1024]{1,0:T(8,128)(2,1)S(1)} %slice.38), channel_id=1, source_target_pairs={{0,2},{1,3},{2,0},{3,1},{4,6},{5,7},{6,4},{7,5},{8,10},{9,11},{10,... | collective-permute-start | bytes 393224 | tf_op jit(solution)/shard_map/ppermute | solution.py:184
  22.4 5.7 %copy-start.2 = (bf16[32,1024]{1,0:T(8,128)(2,1)}, bf16[32,1024]{1,0:T(8,128)(2,1)S(1)}, u32[]{:S(2)}) copy-start(bf16[32,1024]{1,0:T(8,128)(2,1)S(1)} %collective-permute-done.5.refs_2_) | copy-start | bytes 196612
  22.5 5.7 %collective-permute-start.6 = (bf16[64,1024]{1,0:T(8,128)(2,1)S(1)}, bf16[64,1024]{1,0:T(8,128)(2,1)S(1)}, u32[]{:S(2)}, u32[]{:S(2)}) collective-permute-start(bf16[64,1024]{1,0:T(8,128)(2,1)S(1)} %pad_maximum_fusion.1), channel_id=1, source_target_pairs={{0,2},{1,3},{2,0},{3,1},{4,6},{5,7},{6,4},{7,5},{8,10},{9,11},{10,... | collective-permute-start | bytes 393224 | tf_op jit(solution)/shard_map/ppermute | solution.py:184
  26.8 4.3 %collective-permute-start.2 = (bf16[32,1024]{1,0:T(8,128)(2,1)S(1)}, bf16[32,1024]{1,0:T(8,128)(2,1)S(1)}, u32[]{:S(2)}, u32[]{:S(2)}) collective-permute-start(bf16[32,1024]{1,0:T(8,128)(2,1)S(1)} %slice.39), channel_id=1, source_target_pairs={{0,4},{1,5},{2,6},{3,7},{4,0},{5,1},{6,2},{7,3},{8,12},{9,13},{10,... | collective-permute-start | bytes 196616 | tf_op jit(solution)/shard_map/ppermute | solution.py:184
  28.1 0.7 %copy-start.3 = (bf16[64,1024]{1,0:T(8,128)(2,1)}, bf16[64,1024]{1,0:T(8,128)(2,1)S(1)}, u32[]{:S(2)}) copy-start(bf16[64,1024]{1,0:T(8,128)(2,1)S(1)} %collective-permute-done.6.refs_3_) | copy-start | bytes 393220
  28.8 6.6 %collective-permute-start.7 = (bf16[128,1024]{1,0:T(8,128)(2,1)S(1)}, bf16[128,1024]{1,0:T(8,128)(2,1)S(1)}, u32[]{:S(2)}, u32[]{:S(2)}) collective-permute-start(bf16[128,1024]{1,0:T(8,128)(2,1)S(1)} %pad_maximum_fusion), channel_id=1, source_target_pairs={{0,1},{1,0},{2,3},{3,2},{4,5},{5,4},{6,7},{7,6},{8,9},{9,8},{10,11... | collective-permute-start | bytes 786440 | tf_op jit(solution)/shard_map/ppermute | solution.py:184
  31.8 11.3 %collective-permute-start.3 = (bf16[16,1024]{1,0:T(8,128)(2,1)S(1)}, bf16[16,1024]{1,0:T(8,128)(2,1)S(1)}, u32[]{:S(2)}, u32[]{:S(2)}) collective-permute-start(bf16[16,1024]{1,0:T(8,128)(2,1)S(1)} %slice.40), channel_id=1, source_target_pairs={{0,8},{1,9},{2,10},{3,11},{4,12},{5,13},{6,14},{7,15},{8,0},{9,1},... | collective-permute-start | bytes 98312 | tf_op jit(solution)/shard_map/ppermute | solution.py:184
  35.4 0.7 %copy-start.6 = (bf16[128,1024]{1,0:T(8,128)(2,1)}, bf16[128,1024]{1,0:T(8,128)(2,1)S(1)}, u32[]{:S(2)}) copy-start(bf16[128,1024]{1,0:T(8,128)(2,1)S(1)} %collective-permute-done.7.refs_4_) | copy-start | bytes 786436
  43.0 0.6 %copy-start.4 = (bf16[16,1024]{1,0:T(8,128)(2,1)}, bf16[16,1024]{1,0:T(8,128)(2,1)S(1)}, u32[]{:S(2)}) copy-start(bf16[16,1024]{1,0:T(8,128)(2,1)S(1)} %collective-permute-done.3.got_ref) | copy-start | bytes 98308

commit v2 on v1

v2 whole, which is shorter than its diff:
```python
import functools

import jax
import jax.numpy as jnp
from jax import lax
from jax.experimental import pallas as pl
from jax.experimental.pallas import tpu as pltpu
from jax.sharding import PartitionSpec as P

F32 = jnp.float32
BF16 = jnp.bfloat16
NT = (((1,), (1,)), ((), ()))
PARAMS = pltpu.CompilerParams(vmem_limit_bytes=24 * 1024 * 1024)


def iota(shape, axis):
    return lax.broadcasted_iota(jnp.int32, shape, axis)


def own_presence(mask, me, rows):
    pick = iota((mask.shape[1], rows), 0) == me * rows + iota((mask.shape[1], rows), 1)
    return jnp.dot(mask.astype(F32).astype(BF16), pick.astype(F32).astype(BF16), preferred_element_type=F32)


def presence_row(own, sequence_major):
    depth, rows = own.shape
    count = depth * rows
    column = iota((rows, count), 1)
    residue = column % rows if sequence_major else column // depth
    spread = (residue == iota((rows, count), 0)).astype(F32).astype(BF16)
    wide = jnp.dot(own.astype(BF16), spread, preferred_element_type=F32)
    column = iota((depth, count), 1)
    sequence = column // rows if sequence_major else column % depth
    return jnp.sum(jnp.where(sequence == iota((depth, count), 0), wide, 0.0), axis=0, keepdims=True)


def project_kernel(
    rows,
    x_far, mask_far, res_far, lw_far, rw_far, ow_far, g_far,
    left_ref, right_ref, x_ref, mask_ref, lw_ref, rw_ref, owp_ref, stack_ref, inverse_ref, g_ref,
    res_ref, ow_ref, normed, flat, ow_wide, arrived,
):
    sources = (x_far, mask_far, res_far, lw_far, rw_far, ow_far, g_far)
    targets = (x_ref, mask_ref, res_ref, lw_ref, rw_ref, ow_ref, g_ref)
    copies = [pltpu.make_async_copy(a, b, arrived.at[t]) for t, (a, b) in enumerate(zip(sources, targets))]
    for copy in copies:
        copy.start()
    for copy in copies[:-1]:
        copy.wait()
    count, channels = x_ref.shape
    depth, width = mask_ref.shape
    hidden = lw_ref.shape[0]
    pair = ow_ref.shape[1]
    me = lax.axis_index("row")
    value = x_ref[...].astype(F32)
    centered = value - jnp.mean(value, axis=-1, keepdims=True)
    recip = lax.rsqrt(jnp.mean(centered * centered, axis=-1, keepdims=True) + 1e-05)
    value = centered * recip
    normed[...] = value
    own = own_presence(mask_ref[...], me, rows)
    right = lax.dot_general(rw_ref[...], value.astype(BF16), NT, preferred_element_type=F32)
    right = right * presence_row(own, True)
    for s in range(depth):
        flat[pl.ds(s, hidden, stride=depth), :] = right[:, s * rows : (s + 1) * rows]
    right_ref[...] = flat[...].T.astype(BF16)
    by_residue = jnp.concatenate(
        [normed[pl.ds(i, depth, stride=rows), :] for i in range(rows)], axis=0
    ).astype(BF16)
    left = lax.dot_general(lw_ref[...], by_residue, NT, preferred_element_type=F32)
    left_ref[...] = (left * presence_row(own, False)).astype(BF16)
    mask = mask_ref[...].astype(F32)
    residue = res_ref[...].astype(F32)
    residue_own = own_presence(jnp.broadcast_to(res_ref[...], (8, width)), me, rows)[:1]
    tall = jnp.concatenate([mask, jnp.broadcast_to(residue, (8, width))], axis=0).T
    counts = jnp.dot(tall[:, :depth].astype(BF16), own.astype(BF16), preferred_element_type=F32) + 0.001
    inverse_ref[...] = tall[:, depth : depth + 1] * residue_own / counts
    ow_wide[...] = ow_ref[...].astype(F32)
    for e in range(hidden):
        owp_ref[e * hidden : (e + 1) * hidden, :] = ow_wide[pl.ds(e, hidden, stride=hidden), :].astype(BF16)
    for g in range(hidden * hidden // 256):
        stack_ref[g * pair : (g + 1) * pair, :] = owp_ref[g * 256 : (g + 1) * 256, :].T
    copies[-1].wait()


def spread_kernel(rows, size, g_ref, inverse_ref, left_ref, stack_ref, scaled_ref, spread_ref):
    hidden, count = left_ref.shape
    depth = count // rows
    pair = g_ref.shape[2]
    me = lax.axis_index("row")
    bits = size.bit_length() - 1
    fold = 256 // hidden
    groups = hidden // fold
    per = 128 // depth
    blocks = rows // per
    tile = jnp.concatenate([left_ref[:, g * 128 : (g + 1) * 128] for g in range(blocks)], axis=0)
    column = iota((128, per * 256), 1)
    repeat = (column % depth + depth * (column // 256)) == iota((128, per * 256), 0)
    wide = jnp.dot(tile, repeat.astype(F32).astype(BF16), preferred_element_type=F32)
    diagonal = iota((256, 256), 0) // hidden == iota((256, 256), 1) // depth
    for i in range(rows):
        g, q = divmod(i, per)
        own_left = wide[g * hidden : (g + 1) * hidden, q * 256 : (q + 1) * 256]
        block = jnp.where(diagonal, jnp.concatenate([own_left] * fold, axis=0), 0.0).astype(BF16)
        out = jnp.dot(stack_ref[...], block, preferred_element_type=F32).astype(BF16)
        for g in range(groups):
            spread_ref[i * pair : (i + 1) * pair, g * 256 : (g + 1) * 256] = out[g * pair : (g + 1) * pair, :]
        for p in range(i * size // rows, (i + 1) * size // rows):
            relative = sum(((p >> (bits - 1 - t)) & 1) << t for t in range(bits))
            begin = pl.multiple_of((me ^ relative) * rows, rows)
            factor = inverse_ref[pl.ds(begin, rows), :]
            for h in range(rows):
                part = g_ref[h, pl.ds(begin, rows), :].astype(F32) * factor[:, h : h + 1]
                scaled_ref[p * rows : (p + 1) * rows, h * pair : (h + 1) * pair] = part.astype(BF16)


def send_kernel(scaled_ref, spread_ref, send_ref):
    half = send_ref.shape[0]
    send_ref[...] = jnp.dot(scaled_ref[half:, :], spread_ref[...], preferred_element_type=F32).astype(BF16)


def keep_kernel(rows, scaled_ref, spread_ref, x_ref, mask_ref, keep_ref, normed_ref, recip_ref, presence_ref):
    half = keep_ref.shape[0]
    keep_ref[...] = jnp.dot(scaled_ref[:half, :], spread_ref[...], preferred_element_type=F32)
    value = x_ref[...].astype(F32).T
    centered = value - jnp.mean(value, axis=0, keepdims=True)
    recip = lax.rsqrt(jnp.mean(centered * centered, axis=0, keepdims=True) + 1e-05)
    normed_ref[...] = centered * recip
    recip_ref[...] = recip
    presence_ref[...] = presence_row(own_presence(mask_ref[...], lax.axis_index("row"), rows), True)


def left_kernel(rows, near_ref, far_ref, scaled_ref, owp_ref, lw_ref, grad_ref, turned, outer, total):
    hidden = lw_ref.shape[0]
    count = total.shape[0]
    depth = count // rows
    pair = owp_ref.shape[1]
    half = near_ref.shape[0]
    turned[:, :half] = near_ref[...].T
    turned[:, half:] = far_ref[...].T
    for q in range(rows // 2):
        out = jnp.dot(
            turned[...], scaled_ref[:, q * 2 * pair : (q + 1) * 2 * pair], preferred_element_type=F32
        ).astype(BF16)
        for h in range(2):
            i = 2 * q + h
            outer[:, i * depth : (i + 1) * depth, :] = out[:, h * pair : (h + 1) * pair].reshape(hidden, depth, pair)
    acc = jnp.zeros((count, hidden), F32)
    for e in range(0, hidden, 2):
        lhs = jnp.concatenate([outer[e], outer[e + 1]], axis=1)
        rhs = jnp.concatenate(
            [owp_ref[e * hidden : (e + 1) * hidden, :], owp_ref[(e + 1) * hidden : (e + 2) * hidden, :]], axis=1
        )
        acc = acc + lax.dot_general(lhs, rhs, NT, preferred_element_type=F32)
    total[...] = acc
    by_sequence = jnp.concatenate([total[pl.ds(s, rows, stride=depth), :] for s in range(depth)], axis=0)
    grad_ref[...] = lax.dot_general(
        lw_ref[...].astype(F32).T, by_sequence, NT, preferred_element_type=F32, precision=lax.Precision.HIGHEST
    )


def final_kernel(rows, keep_ref, got_ref, rw_ref, grad_ref, normed_ref, recip_ref, presence_ref, out_ref, flat, lanes):
    hidden = rw_ref.shape[0]
    depth = keep_ref.shape[1] // hidden
    flat[...] = (keep_ref[...] + got_ref[...].astype(F32)).T
    for s in range(depth):
        lanes[:, s * rows : (s + 1) * rows] = flat[pl.ds(s, hidden, stride=depth), :]
    grad = jnp.dot(
        rw_ref[...].astype(F32).T, lanes[...], preferred_element_type=F32, precision=lax.Precision.HIGHEST
    )
    grad = (grad + grad_ref[...]) * presence_ref[...]
    normed = normed_ref[...]
    mean = jnp.mean(grad, axis=0, keepdims=True)
    cross = jnp.mean(grad * normed, axis=0, keepdims=True)
    out_ref[...] = (recip_ref[...] * (grad - mean - normed * cross)).T


def near_shape(dims, dtype):
    return pltpu.VMEM(dims, dtype)


def near(value):
    return pltpu.with_memory_space_constraint(value, pltpu.VMEM)


def far(value):
    return pltpu.with_memory_space_constraint(value, pltpu.HBM)


def call(kernel, name, out_shape, args, scratch=(), flops=0, in_specs=None):
    vmem = pl.BlockSpec(memory_space=pltpu.VMEM)
    out_specs = (vmem,) * len(out_shape) if isinstance(out_shape, tuple) else vmem
    return pl.pallas_call(
        kernel,
        out_shape=out_shape,
        in_specs=in_specs or [vmem] * len(args),
        out_specs=out_specs,
        scratch_shapes=scratch,
        compiler_params=PARAMS,
        cost_estimate=pl.CostEstimate(flops=flops, bytes_accessed=1 << 20, transcendentals=0),
        name=name,
    )(*args)


def shards(size, x, mask, residue_mask, lw, rw, ow, g):
    depth, rows, channels = x.shape
    hidden = lw.shape[1]
    width, pair = g.shape[1:]
    count = depth * rows
    flat_width = depth * hidden

    def exchange(value, bit):
        return lax.ppermute(value, "row", [(d, d ^ bit) for d in range(size)])

    sources = (x.reshape(count, channels), mask, residue_mask.reshape(1, width), lw.T, rw.T, ow, g)
    left, right, x, mask, lw, rw, owp, stack, inverse, g = call(
        functools.partial(project_kernel, rows),
        "project",
        (
            near_shape((hidden, count), BF16),
            near_shape((rows, flat_width), BF16),
            near_shape((count, channels), BF16),
            near_shape(mask.shape, mask.dtype),
            near_shape((hidden, channels), BF16),
            near_shape((hidden, channels), BF16),
            near_shape(ow.shape, BF16),
            near_shape((ow.shape[0] // 256 * pair, 256), BF16),
            near_shape((width, rows), F32),
            near_shape(g.shape, BF16),
        ),
        [far(v) for v in sources],
        [
            pltpu.VMEM((1, width), residue_mask.dtype),
            pltpu.VMEM(ow.shape, BF16),
            pltpu.VMEM((count, channels), F32),
            pltpu.VMEM((flat_width, rows), F32),
            pltpu.VMEM(ow.shape, F32),
            pltpu.SemaphoreType.DMA((len(sources),)),
        ],
        in_specs=[pl.BlockSpec(memory_space=pl.ANY)] * len(sources),
    )
    block = right
    bits = [1 << t for t in range(size.bit_length() - 1)]
    gathers = bits[::-1]

    def gather(block):
        return exchange(block, gathers.pop(0))

    early = gather(block)
    scaled, spread = call(
        functools.partial(spread_kernel, rows, size),
        "spread",
        (near_shape((width, rows * pair), BF16), near_shape((rows * pair, flat_width), BF16)),
        [near(v) for v in (g, inverse, left, stack)],
        flops=2 * 2**30,
    )
    early, spread = lax.optimization_barrier((early, spread))
    block = jnp.concatenate([block, early], axis=0)
    early = gather(block)
    send = call(
        send_kernel,
        "send",
        near_shape((width // 2, flat_width), BF16),
        [near(scaled), near(spread)],
        flops=2**30,
    )
    got = exchange(send, bits[0])
    keep, normed, recip, presence = call(
        functools.partial(keep_kernel, rows),
        "keep",
        (
            near_shape((width // 2, flat_width), F32),
            near_shape((channels, count), F32),
            near_shape((1, count), F32),
            near_shape((1, count), F32),
        ),
        [near(v) for v in (scaled, spread, x, mask)],
        flops=2**30,
    )
    for bit in bits[1:]:
        total = keep + got.astype(F32)
        half = total.shape[0] // 2
        keep = total[:half]
        got = exchange(total[half:].astype(BF16), bit)
        if block.shape[0] < width // 2:
            block = jnp.concatenate([block, early], axis=0)
            early = gather(block)
    while block.shape[0] < width // 2:
        block = jnp.concatenate([block, early], axis=0)
        early = gather(block)
    grad = call(
        functools.partial(left_kernel, rows),
        "left",
        near_shape((channels, count), F32),
        [near(v) for v in (block, early, scaled, owp, lw)],
        [
            pltpu.VMEM((flat_width, width), BF16),
            pltpu.VMEM((hidden, count, pair), BF16),
            pltpu.VMEM((count, hidden), F32),
        ],
        flops=4 * 2**30,
    )
    out = call(
        functools.partial(final_kernel, rows),
        "final",
        jax.ShapeDtypeStruct((count, channels), F32),
        [near(v) for v in (keep, got, rw, grad, normed, recip, presence)],
        [pltpu.VMEM((flat_width, rows), F32), pltpu.VMEM((hidden, count), F32)],
    )
    return out.reshape(depth, rows, channels)


def solution(mesh):
    return jax.shard_map(
        functools.partial(shards, mesh.shape["row"]),
        mesh=mesh,
        in_specs=(
            P("groups", "row", None),
            P("groups", None),
            P("groups"),
            P(),
            P(),
            P(),
            P(("groups", "row"), None, None),
        ),
        out_specs=P("groups", "row", None),
        check_vma=False,
    )
```

time: 46.6 us -> 33.1 us (0.71)
  Pallas kernels: 19.3 us -> 12.1 us
  local copies, waits for them, and re-layouts: 4.67 us -> 0.06 us
  other arithmetic: 1.18 us -> 0.12 us
  starting transfers between devices: 13.5 us -> 12.6 us
    pallas_call x4 -> x6, Pallas kernels: 19.3 us -> 12.1 us  [call(): pl.pallas_call(kernel, out_shape=out_shape, in_specs=in_specs or [vmem] *...]
    unnamed x16 -> x3, local copies, waits for them, and re-layouts: 4.01 us -> 0.01 us
    add x3, other arithmetic: 1.15 us -> 0.1 us  [shards(): total = keep + got.astype(F32)]
    ppermute x8, starting transfers between devices: 13.5 us -> 12.6 us  [exchange(): return lax.ppermute(value, 'row', [(d, d ^ bit) for d in range(size)])]
    slice x1, local copies, waits for them, and re-layouts: 0.63 us -> 0.01 us  [shards(): keep = total[:half]]
  transfers between devices with their start and end apart: 8 -> 8, of which waited for: 4 -> 5; matrix products, arithmetic and copies ran while one was open for 4% -> 1% of each run, Pallas kernels for 15% -> 21%
where the time goes in v2:
time: 33.1 us; the launch traced here: 33 us
  starting transfers between devices  12.6 us (38%)
  Pallas kernels  12.1 us (37%)
  waiting for transfers between devices  7.94 us (24%)
    ppermute x8, starting transfers between devices, exchange(): return lax.ppermute(value, 'row', [(d, d ^ bit) for d in range(size)])  12.6 us
    pallas_call x6, Pallas kernels, call(): pl.pallas_call(kernel, out_shape=out_shape, in_specs=in_specs or [vmem] *...  12.1 us
    ppermute x8, waiting for transfers between devices, exchange(): return lax.ppermute(value, 'row', [(d, d ^ bit) for d in range(size)])  7.94 us
  transfers between devices with their start and end apart: 8, of which 5 were waited for; matrix products, arithmetic and copies ran while one was open for 1% of the time, Pallas kernels for 21%

profile of v2, /device:TPU:0, one launch (start us, length us, event | category | flops | bytes accessed | tf_op | source)
XLA Modules:
  0.0 33.0 jit_solution(11434888408450511542)
XLA Ops:
  0.0 2.6 %project.1 = (bf16[32,512]{1,0:T(8,128)(2,1)S(1)}, bf16[16,1024]{1,0:T(8,128)(2,1)S(1)}, bf16[512,64]{1,0:T(8,128)(2,1)S(1)}, s32[32,256]{1,0:T(8,128)S(1)}, bf1...) custom-call(bf16[512,64]{1,0:T(8,128)(2,1)} %bitcast.5, ...), custom_call_target="tpu_custom_call" | custom-call | bytes 1048576 | tf_op jit(solution)/shard_map/project/pallas_call | solution.py:192
  2.7 4.1 %collective-permute-start = (bf16[16,1024]{1,0:T(8,128)(2,1)S(1)}, bf16[16,1024]{1,0:T(8,128)(2,1)S(1)}, u32[]{:S(2)}, u32[]{:S(2)}) collective-permute-start(bf16[16,1024]{1,0:T(8,128)(2,1)S(1)} %get-tuple-element.28), channel_id=1, source_target_pairs={{0,8},{1,9},{2,10},{3,11},{4,12},{5,13},{6,14},{7,15},{8,0},{9,1},... | collective-permute-start | bytes 98312 | tf_op jit(solution)/shard_map/ppermute | solution.py:212
  6.8 1.4 %spread.1 = (bf16[256,2048]{1,0:T(8,128)(2,1)S(1)}, bf16[2048,1024]{1,0:T(8,128)(2,1)S(1)}) custom-call(bf16[16,256,128]{2,1,0:T(8,128)(2,1)S(1)} %get-tuple-element.23.g_ref, f32[256,16]{1,0:T(8,128)S(1)} %get-tuple-element.24.inverse_ref, bf16[32,512]{1,0:T(8,128)(2,1)S(1)} %get-tuple-element.25.left_ref, bf16[512,256]{1,0:T(8,128)(2,1)S(1)} %get-tuple-element.26.stack_ref), custom_call_target="tpu_custom_call" | custom-call | flops 2147483648 | bytes 1048576 | tf_op jit(solution)/shard_map/spread/pallas_call | solution.py:192
  8.2 0.8 %collective-permute-done = bf16[16,1024]{1,0:T(8,128)(2,1)S(1)} collective-permute-done((bf16[16,1024]{1,0:T(8,128)(2,1)S(1)}, bf16[16,1024]{1,0:T(8,128)(2,1)S(1)}, u32[]{:S(2)}, u32[]{:S(2)}) %collective-permute-start) | collective-permute-done | bytes 32800 | tf_op jit(solution)/shard_map/ppermute | solution.py:212
  9.0 0.7 %send.1 = bf16[128,1024]{1,0:T(8,128)(2,1)S(1)} custom-call(bf16[256,2048]{1,0:T(8,128)(2,1)S(1)} %get-tuple-element.27.scaled_ref, bf16[2048,1024]{1,0:T(8,128)(2,1)S(1)} %get-tuple-element.30.spread_ref), custom_call_target="tpu_custom_call" | custom-call | flops 1073741824 | bytes 1048576 | tf_op jit(solution)/shard_map/send/pallas_call | solution.py:192
  9.7 0.1 collective-permute-start.1
  9.8 1.6 %collective-permute-start.5 = (bf16[32,1024]{1,0:T(8,128)(2,1)S(1)}, bf16[32,1024]{1,0:T(8,128)(2,1)S(1)}, u32[]{:S(2)}, u32[]{:S(2)}) collective-permute-start(bf16[32,1024]{1,0:T(8,128)(2,1)S(1)} %pad_maximum_fusion.1), channel_id=1, source_target_pairs={{0,4},{1,5},{2,6},{3,7},{4,0},{5,1},{6,2},{7,3},{8,12},{9,13},{10,... | collective-permute-start | bytes 196616 | tf_op jit(solution)/shard_map/ppermute | solution.py:212
  11.5 0.9 %keep.1 = (f32[128,1024]{1,0:T(8,128)S(1)}, f32[64,512]{1,0:T(8,128)S(1)}, f32[1,512]{1,0:T(1,128)S(1)}, f32[1,512]{1,0:T(1,128)S(1)}) custom-call(bf16[256,2048]{1,0:T(8,128)(2,1)S(1)} %get-tuple-element.27.scaled_ref, bf16[2048,1024]{1,0:T(8,128)(2,1)S(1)} %get-tuple-element.30.spread_ref, bf16[512,64]{1,0:T(8,128)(2,1)S(1)} %get-tuple-element.31.x_ref, ...), custom_call_target="tpu_custom_call" | custom-call | flops 1073741824 | bytes 1048576 | tf_op jit(solution)/shard_map/keep/pallas_call | solution.py:192
  12.3 0.0 collective-permute-done.1
  12.4 0.1 convert_add_fusion
  12.4 1.6 %collective-permute-start.2 = (bf16[64,1024]{1,0:T(8,128)(2,1)S(1)}, bf16[64,1024]{1,0:T(8,128)(2,1)S(1)}, u32[]{:S(2)}, u32[]{:S(2)}) collective-permute-start(bf16[64,1024]{1,0:T(8,128)(2,1)S(1)} %slice.38), channel_id=1, source_target_pairs={{0,2},{1,3},{2,0},{3,1},{4,6},{5,7},{6,4},{7,5},{8,10},{9,11},{10,... | collective-permute-start | bytes 393224 | tf_op jit(solution)/shard_map/ppermute | solution.py:212
  14.0 0.3 collective-permute-done.5
  14.3 1.8 %collective-permute-start.6 = (bf16[64,1024]{1,0:T(8,128)(2,1)S(1)}, bf16[64,1024]{1,0:T(8,128)(2,1)S(1)}, u32[]{:S(2)}, u32[]{:S(2)}) collective-permute-start(bf16[64,1024]{1,0:T(8,128)(2,1)S(1)} %pad_maximum_fusion), channel_id=1, source_target_pairs={{0,2},{1,3},{2,0},{3,1},{4,6},{5,7},{6,4},{7,5},{8,10},{9,11},{10,... | collective-permute-start | bytes 393224 | tf_op jit(solution)/shard_map/ppermute | solution.py:212
  16.1 2.7 %collective-permute-done.2 = bf16[64,1024]{1,0:T(8,128)(2,1)S(1)} collective-permute-done((bf16[64,1024]{1,0:T(8,128)(2,1)S(1)}, bf16[64,1024]{1,0:T(8,128)(2,1)S(1)}, u32[]{:S(2)}, u32[]{:S(2)}) %collective-permute-start.2) | collective-permute-done | bytes 131104 | tf_op jit(solution)/shard_map/ppermute | solution.py:212
  18.9 0.1 collective-permute-start.3
  19.0 1.9 %collective-permute-done.6 = bf16[64,1024]{1,0:T(8,128)(2,1)S(1)} collective-permute-done((bf16[64,1024]{1,0:T(8,128)(2,1)S(1)}, bf16[64,1024]{1,0:T(8,128)(2,1)S(1)}, u32[]{:S(2)}, u32[]{:S(2)}) %collective-permute-start.6) | collective-permute-done | bytes 131104 | tf_op jit(solution)/shard_map/ppermute | solution.py:212
  20.9 0.1 collective-permute-start.7
  21.0 2.3 %collective-permute-done.3 = bf16[32,1024]{1,0:T(8,128)(2,1)S(1)} collective-permute-done((bf16[32,1024]{1,0:T(8,128)(2,1)S(1)}, bf16[32,1024]{1,0:T(8,128)(2,1)S(1)}, u32[]{:S(2)}, u32[]{:S(2)}) %collective-permute-start.3) | collective-permute-done | bytes 65568 | tf_op jit(solution)/shard_map/ppermute | solution.py:212
  23.3 3.2 %collective-permute-start.4 = (bf16[16,1024]{1,0:T(8,128)(2,1)S(1)}, bf16[16,1024]{1,0:T(8,128)(2,1)S(1)}, u32[]{:S(2)}, u32[]{:S(2)}) collective-permute-start(bf16[16,1024]{1,0:T(8,128)(2,1)S(1)} %slice.40), channel_id=1, source_target_pairs={{0,8},{1,9},{2,10},{3,11},{4,12},{5,13},{6,14},{7,15},{8,0},{9,1},... | collective-permute-start | bytes 98312 | tf_op jit(solution)/shard_map/ppermute | solution.py:212
  26.5 0.0 collective-permute-done.7.far_ref
  26.5 4.8 %left.1.grad_ref = f32[64,512]{1,0:T(8,128)S(1)} custom-call(bf16[128,1024]{1,0:T(8,128)(2,1)S(1)} %constant_dynamic-update-slice_fusion.near_ref, bf16[128,1024]{1,0:T(8,128)(2,1)S(1)} %collective-permute-done.7.far_ref, bf16[256,2048]{1,0:T(8,128)(2,1)S(1)} %get-tuple-element.27.scaled_ref, bf16[1024,128]{1,0:T(8,128)(2,1)S(1)} %get-tuple-element.36.owp_ref, ...), custom_call_target="tpu_custom_call" | custom-call | flops 4294967296 | bytes 1048576 | tf_op jit(solution)/shard_map/left/pallas_call | solution.py:192
  31.3 0.0 collective-permute-done.4.got_ref
  31.3 1.7 %final.1 = f32[512,64]{1,0:T(8,128)} custom-call(f32[16,1024]{1,0:T(8,128)S(1)} %slice.31.keep_ref, bf16[16,1024]{1,0:T(8,128)(2,1)S(1)} %collective-permute-done.4.got_ref, bf16[32,64]{1,0:T(8,128)(2,1)S(1)} %get-tuple-element.34.rw_ref, f32[64,512]{1,0:T(8,128)S(1)} %left.1.grad_ref, f32[64,512]{1,0:T(8,128)S(1)} %get-tuple-element.38.normed_ref, ...), custom_call_target="tpu_custom_call" | custom-call | bytes 1048576 | tf_op jit(solution)/shard_map/final/pallas_call | solution.py:192
  (12 shorter events, 0.1 us)
Async XLA Ops:
  2.7 6.3 %collective-permute-start = (bf16[16,1024]{1,0:T(8,128)(2,1)S(1)}, bf16[16,1024]{1,0:T(8,128)(2,1)S(1)}, u32[]{:S(2)}, u32[]{:S(2)}) collective-permute-start(bf16[16,1024]{1,0:T(8,128)(2,1)S(1)} %get-tuple-element.28), channel_id=1, source_target_pairs={{0,8},{1,9},{2,10},{3,11},{4,12},{5,13},{6,14},{7,15},{8,0},{9,1},... | collective-permute-start | bytes 98312 | tf_op jit(solution)/shard_map/ppermute | solution.py:212
  9.7 2.6 %collective-permute-start.1 = (bf16[128,1024]{1,0:T(8,128)(2,1)S(1)}, bf16[128,1024]{1,0:T(8,128)(2,1)S(1)}, u32[]{:S(2)}, u32[]{:S(2)}) collective-permute-start(bf16[128,1024]{1,0:T(8,128)(2,1)S(1)} %send.1), channel_id=1, source_target_pairs={{0,1},{1,0},{2,3},{3,2},{4,5},{5,4},{6,7},{7,6},{8,9},{9,8},{10,11... | collective-permute-start | bytes 786440 | tf_op jit(solution)/shard_map/ppermute | solution.py:212
  9.8 4.5 %collective-permute-start.5 = (bf16[32,1024]{1,0:T(8,128)(2,1)S(1)}, bf16[32,1024]{1,0:T(8,128)(2,1)S(1)}, u32[]{:S(2)}, u32[]{:S(2)}) collective-permute-start(bf16[32,1024]{1,0:T(8,128)(2,1)S(1)} %pad_maximum_fusion.1), channel_id=1, source_target_pairs={{0,4},{1,5},{2,6},{3,7},{4,0},{5,1},{6,2},{7,3},{8,12},{9,13},{10,... | collective-permute-start | bytes 196616 | tf_op jit(solution)/shard_map/ppermute | solution.py:212
  12.4 6.4 %collective-permute-start.2 = (bf16[64,1024]{1,0:T(8,128)(2,1)S(1)}, bf16[64,1024]{1,0:T(8,128)(2,1)S(1)}, u32[]{:S(2)}, u32[]{:S(2)}) collective-permute-start(bf16[64,1024]{1,0:T(8,128)(2,1)S(1)} %slice.38), channel_id=1, source_target_pairs={{0,2},{1,3},{2,0},{3,1},{4,6},{5,7},{6,4},{7,5},{8,10},{9,11},{10,... | collective-permute-start | bytes 393224 | tf_op jit(solution)/shard_map/ppermute | solution.py:212
  14.3 6.5 %collective-permute-start.6 = (bf16[64,1024]{1,0:T(8,128)(2,1)S(1)}, bf16[64,1024]{1,0:T(8,128)(2,1)S(1)}, u32[]{:S(2)}, u32[]{:S(2)}) collective-permute-start(bf16[64,1024]{1,0:T(8,128)(2,1)S(1)} %pad_maximum_fusion), channel_id=1, source_target_pairs={{0,2},{1,3},{2,0},{3,1},{4,6},{5,7},{6,4},{7,5},{8,10},{9,11},{10,... | collective-permute-start | bytes 393224 | tf_op jit(solution)/shard_map/ppermute | solution.py:212
  18.9 4.3 %collective-permute-start.3 = (bf16[32,1024]{1,0:T(8,128)(2,1)S(1)}, bf16[32,1024]{1,0:T(8,128)(2,1)S(1)}, u32[]{:S(2)}, u32[]{:S(2)}) collective-permute-start(bf16[32,1024]{1,0:T(8,128)(2,1)S(1)} %slice.39), channel_id=1, source_target_pairs={{0,4},{1,5},{2,6},{3,7},{4,0},{5,1},{6,2},{7,3},{8,12},{9,13},{10,... | collective-permute-start | bytes 196616 | tf_op jit(solution)/shard_map/ppermute | solution.py:212
  20.9 5.6 %collective-permute-start.7 = (bf16[128,1024]{1,0:T(8,128)(2,1)S(1)}, bf16[128,1024]{1,0:T(8,128)(2,1)S(1)}, u32[]{:S(2)}, u32[]{:S(2)}) collective-permute-start(bf16[128,1024]{1,0:T(8,128)(2,1)S(1)} %constant_dynamic-update-slice_fusion.near_ref), channel_id=1, source_target_pairs={{0,1},{1,0},{2,3},{3,2},{4,5},{5,4},{6,7},{7,6},{8,9},{9,8},{10,11... | collective-permute-start | bytes 786440 | tf_op jit(solution)/shard_map/ppermute | solution.py:212
  23.3 8.0 %collective-permute-start.4 = (bf16[16,1024]{1,0:T(8,128)(2,1)S(1)}, bf16[16,1024]{1,0:T(8,128)(2,1)S(1)}, u32[]{:S(2)}, u32[]{:S(2)}) collective-permute-start(bf16[16,1024]{1,0:T(8,128)(2,1)S(1)} %slice.40), channel_id=1, source_target_pairs={{0,8},{1,9},{2,10},{3,11},{4,12},{5,13},{6,14},{7,15},{8,0},{9,1},... | collective-permute-start | bytes 98312 | tf_op jit(solution)/shard_map/ppermute | solution.py:212

commit v3 on v2

--- a/solution.py
+++ b/solution.py
@@ -129,11 +129,18 @@
     presence_ref[...] = presence_row(own_presence(mask_ref[...], lax.axis_index("row"), rows), True)
 
 
-def left_kernel(rows, near_ref, far_ref, scaled_ref, owp_ref, lw_ref, grad_ref, turned, outer, total):
-    hidden = lw_ref.shape[0]
-    count = total.shape[0]
+def weigh(weight, value):
+    high = value.astype(BF16)
+    low = (value - high.astype(F32)).astype(BF16)
+    turned = weight.astype(F32).T.astype(BF16)
+    return jnp.dot(
+        jnp.concatenate([turned, turned], axis=1), jnp.concatenate([high, low], axis=0), preferred_element_type=F32
+    )
+
+
+def outer_kernel(rows, near_ref, far_ref, scaled_ref, outer_ref, turned):
+    hidden, count, pair = outer_ref.shape
     depth = count // rows
-    pair = owp_ref.shape[1]
     half = near_ref.shape[0]
     turned[:, :half] = near_ref[...].T
     turned[:, half:] = far_ref[...].T
@@ -143,31 +150,36 @@
         ).astype(BF16)
         for h in range(2):
             i = 2 * q + h
-            outer[:, i * depth : (i + 1) * depth, :] = out[:, h * pair : (h + 1) * pair].reshape(hidden, depth, pair)
+            outer_ref[:, i * depth : (i + 1) * depth, :] = out[:, h * pair : (h + 1) * pair].reshape(hidden, depth, pair)
+
+
+def left_kernel(rows, outer_ref, owp_ref, lw_ref, grad_ref, total):
+    hidden = lw_ref.shape[0]
+    count = total.shape[0]
+    depth = count // rows
     acc = jnp.zeros((count, hidden), F32)
     for e in range(0, hidden, 2):
-        lhs = jnp.concatenate([outer[e], outer[e + 1]], axis=1)
+        lhs = jnp.concatenate([outer_ref[e], outer_ref[e + 1]], axis=1)
         rhs = jnp.concatenate(
             [owp_ref[e * hidden : (e + 1) * hidden, :], owp_ref[(e + 1) * hidden : (e + 2) * hidden, :]], axis=1
         )
         acc = acc + lax.dot_general(lhs, rhs, NT, preferred_element_type=F32)
     total[...] = acc
     by_sequence = jnp.concatenate([total[pl.ds(s, rows, stride=depth), :] for s in range(depth)], axis=0)
-    grad_ref[...] = lax.dot_general(
-        lw_ref[...].astype(F32).T, by_sequence, NT, preferred_element_type=F32, precision=lax.Precision.HIGHEST
-    )
-
-
-def final_kernel(rows, keep_ref, got_ref, rw_ref, grad_ref, normed_ref, recip_ref, presence_ref, out_ref, flat, lanes):
+    grad_ref[...] = weigh(lw_ref[...], by_sequence.T)
+
+
+def final_kernel(rows, keep_ref, *refs):
+    *got_refs, rw_ref, grad_ref, normed_ref, recip_ref, presence_ref, out_ref, flat, lanes = refs
     hidden = rw_ref.shape[0]
     depth = keep_ref.shape[1] // hidden
-    flat[...] = (keep_ref[...] + got_ref[...].astype(F32)).T
+    total = keep_ref[...]
+    for got_ref in got_refs:
+        total = total + got_ref[...].astype(F32)
+    flat[...] = total.T
     for s in range(depth):
         lanes[:, s * rows : (s + 1) * rows] = flat[pl.ds(s, hidden, stride=depth), :]
-    grad = jnp.dot(
-        rw_ref[...].astype(F32).T, lanes[...], preferred_element_type=F32, precision=lax.Precision.HIGHEST
-    )
-    grad = (grad + grad_ref[...]) * presence_ref[...]
+    grad = (weigh(rw_ref[...], lanes[...]) + grad_ref[...]) * presence_ref[...]
     normed = normed_ref[...]
     mean = jnp.mean(grad, axis=0, keepdims=True)
     cross = jnp.mean(grad * normed, axis=0, keepdims=True)
@@ -238,14 +250,28 @@
         ],
         in_specs=[pl.BlockSpec(memory_space=pl.ANY)] * len(sources),
     )
-    block = right
     bits = [1 << t for t in range(size.bit_length() - 1)]
-    gathers = bits[::-1]
-
-    def gather(block):
-        return exchange(block, gathers.pop(0))
-
-    early = gather(block)
+    stages = [bits[:1]] + [bits[t : t + 2] for t in range(1, len(bits), 2)]
+
+    def partners(stage):
+        found = [0]
+        for bit in reversed(stage):
+            found = found + [bit ^ f for f in found]
+        return found
+
+    def gather(blocks, stage):
+        block = jnp.concatenate(blocks, axis=0) if len(blocks) > 1 else blocks[0]
+        return [block] + [exchange(block, other) for other in partners(stage)[:0:-1]][::-1]
+
+    def scatter(total, stage):
+        others = partners(stage)
+        part = total.shape[0] // len(others)
+        got = [
+            exchange(total[t * part : (t + 1) * part].astype(BF16), others[t]) for t in range(len(others) - 1, 0, -1)
+        ]
+        return total[:part], got
+
+    blocks = gather([right], stages[-1])
     scaled, spread = call(
         functools.partial(spread_kernel, rows, size),
         "spread",
@@ -253,9 +279,7 @@
         [near(v) for v in (g, inverse, left, stack)],
         flops=2 * 2**30,
     )
-    early, spread = lax.optimization_barrier((early, spread))
-    block = jnp.concatenate([block, early], axis=0)
-    early = gather(block)
+    blocks, spread = lax.optimization_barrier((blocks, spread))
     send = call(
         send_kernel,
         "send",
@@ -276,34 +300,36 @@
         [near(v) for v in (scaled, spread, x, mask)],
         flops=2**30,
     )
-    for bit in bits[1:]:
-        total = keep + got.astype(F32)
-        half = total.shape[0] // 2
-        keep = total[:half]
-        got = exchange(total[half:].astype(BF16), bit)
-        if block.shape[0] < width // 2:
-            block = jnp.concatenate([block, early], axis=0)
-            early = gather(block)
-    while block.shape[0] < width // 2:
-        block = jnp.concatenate([block, early], axis=0)
-        early = gather(block)
+    got = [got]
+    for number, stage in enumerate(stages[1:], 1):
+        for piece in got:
+            keep = keep + piece.astype(F32)
+        keep, got = scatter(keep, stage)
+        if number < len(stages) - 1:
+            blocks, keep = lax.optimization_barrier((blocks, keep))
+            blocks = gather(blocks, stages[-1 - number])
+    near_block, far_block = gather(blocks, stages[0])
+    outer = call(
+        functools.partial(outer_kernel, rows),
+        "outer",
+        near_shape((hidden, count, pair), BF16),
+        [near(v) for v in (near_block, far_block, scaled)],
+        [pltpu.VMEM((flat_width, width), BF16)],
+        flops=2**26,
+    )
     grad = call(
         functools.partial(left_kernel, rows),
         "left",
         near_shape((channels, count), F32),
-        [near(v) for v in (block, early, scaled, owp, lw)],
-        [
-            pltpu.VMEM((flat_width, width), BF16),
-            pltpu.VMEM((hidden, count, pair), BF16),
-            pltpu.VMEM((count, hidden), F32),
-        ],
-        flops=4 * 2**30,
+        [near(v) for v in (outer, owp, lw)],
+        [pltpu.VMEM((count, hidden), F32)],
+        flops=2**26,
     )
     out = call(
         functools.partial(final_kernel, rows),
         "final",
         jax.ShapeDtypeStruct((count, channels), F32),
-        [near(v) for v in (keep, got, rw, grad, normed, recip, presence)],
+        [near(v) for v in (keep, *got, rw, grad, normed, recip, presence)],
         [pltpu.VMEM((flat_width, rows), F32), pltpu.VMEM((hidden, count), F32)],
     )
     return out.reshape(depth, rows, channels)

time: 33.1 us -> 29.9 us (0.903)
  waiting for transfers between devices: 7.94 us -> 5.2 us
  Pallas kernels: 12.1 us -> 10.1 us
  starting transfers between devices: 12.6 us -> 14.2 us
    ppermute x8 -> x10, waiting for transfers between devices: 7.94 us -> 5.2 us  [exchange(): return lax.ppermute(value, 'row', [(d, d ^ bit) for d in range(size)])]
    pallas_call x6 -> x7, Pallas kernels: 12.1 us -> 10.1 us  [call(): pl.pallas_call(kernel, out_shape=out_shape, in_specs=in_specs or [vmem] *...]
    ppermute x8 -> x10, starting transfers between devices: 12.6 us -> 14.2 us  [exchange(): return lax.ppermute(value, 'row', [(d, d ^ bit) for d in range(size)])]
  transfers between devices with their start and end apart: 8 -> 10, of which waited for: 5 -> 6; matrix products, arithmetic and copies ran while one was open for 1% -> 0% of each run, Pallas kernels for 21% -> 17%
where the time goes in v3:
time: 29.9 us; the launch traced here: 29.8 us
  starting transfers between devices  14.2 us (47%)
  Pallas kernels  10.1 us (34%)
  waiting for transfers between devices  5.2 us (17%)
    ppermute x10, starting transfers between devices, exchange(): return lax.ppermute(value, 'row', [(d, d ^ bit) for d in range(size)])  14.2 us
    pallas_call x7, Pallas kernels, call(): pl.pallas_call(kernel, out_shape=out_shape, in_specs=in_specs or [vmem] *...  10.1 us
    ppermute x10, waiting for transfers between devices, exchange(): return lax.ppermute(value, 'row', [(d, d ^ bit) for d in range(size)])  5.2 us
  transfers between devices with their start and end apart: 10, of which 6 were waited for; matrix products, arithmetic and copies ran while one was open for 0% of the time, Pallas kernels for 17%

profile of v3, /device:TPU:0, one launch (start us, length us, event | category | flops | bytes accessed | tf_op | source)
XLA Modules:
  0.0 29.8 jit_solution(4606386610951113832)
XLA Ops:
  0.0 2.6 %project.1 = (bf16[32,512]{1,0:T(8,128)(2,1)S(1)}, bf16[16,1024]{1,0:T(8,128)(2,1)S(1)}, bf16[512,64]{1,0:T(8,128)(2,1)S(1)}, s32[32,256]{1,0:T(8,128)S(1)}, bf1...) custom-call(bf16[512,64]{1,0:T(8,128)(2,1)} %bitcast.5, ...), custom_call_target="tpu_custom_call" | custom-call | bytes 1048576 | tf_op jit(solution)/shard_map/project/pallas_call | solution.py:204
  2.7 4.1 %collective-permute-start = (bf16[16,1024]{1,0:T(8,128)(2,1)S(1)}, bf16[16,1024]{1,0:T(8,128)(2,1)S(1)}, u32[]{:S(2)}, u32[]{:S(2)}) collective-permute-start(bf16[16,1024]{1,0:T(8,128)(2,1)S(1)} %get-tuple-element.42), channel_id=1, source_target_pairs={{0,8},{1,9},{2,10},{3,11},{4,12},{5,13},{6,14},{7,15},{8,0},{9,1},... | collective-permute-start | bytes 98312 | tf_op jit(solution)/shard_map/ppermute | solution.py:224
  6.8 1.4 %spread.1 = (bf16[256,2048]{1,0:T(8,128)(2,1)S(1)}, bf16[2048,1024]{1,0:T(8,128)(2,1)S(1)}) custom-call(bf16[16,256,128]{2,1,0:T(8,128)(2,1)S(1)} %get-tuple-element.28.g_ref, f32[256,16]{1,0:T(8,128)S(1)} %get-tuple-element.29.inverse_ref, bf16[32,512]{1,0:T(8,128)(2,1)S(1)} %get-tuple-element.30.left_ref, bf16[512,256]{1,0:T(8,128)(2,1)S(1)} %get-tuple-element.31.stack_ref), custom_call_target="tpu_custom_call" | custom-call | flops 2147483648 | bytes 1048576 | tf_op jit(solution)/shard_map/spread/pallas_call | solution.py:204
  8.2 0.8 %collective-permute-done = bf16[16,1024]{1,0:T(8,128)(2,1)S(1)} collective-permute-done((bf16[16,1024]{1,0:T(8,128)(2,1)S(1)}, bf16[16,1024]{1,0:T(8,128)(2,1)S(1)}, u32[]{:S(2)}, u32[]{:S(2)}) %collective-permute-start) | collective-permute-done | bytes 32800 | tf_op jit(solution)/shard_map/ppermute | solution.py:224
  9.0 0.7 %send.1 = bf16[128,1024]{1,0:T(8,128)(2,1)S(1)} custom-call(bf16[256,2048]{1,0:T(8,128)(2,1)S(1)} %get-tuple-element.35.scaled_ref, bf16[2048,1024]{1,0:T(8,128)(2,1)S(1)} %get-tuple-element.36.spread_ref), custom_call_target="tpu_custom_call" | custom-call | flops 1073741824 | bytes 1048576 | tf_op jit(solution)/shard_map/send/pallas_call | solution.py:204
  9.8 0.1 collective-permute-start.1
  9.8 0.9 %keep.1 = (f32[128,1024]{1,0:T(8,128)S(1)}, f32[64,512]{1,0:T(8,128)S(1)}, f32[1,512]{1,0:T(1,128)S(1)}, f32[1,512]{1,0:T(1,128)S(1)}) custom-call(bf16[256,2048]{1,0:T(8,128)(2,1)S(1)} %get-tuple-element.35.scaled_ref, bf16[2048,1024]{1,0:T(8,128)(2,1)S(1)} %get-tuple-element.36.spread_ref, bf16[512,64]{1,0:T(8,128)(2,1)S(1)} %get-tuple-element.37.x_ref, ...), custom_call_target="tpu_custom_call" | custom-call | flops 1073741824 | bytes 1048576 | tf_op jit(solution)/shard_map/keep/pallas_call | solution.py:204
  10.7 0.6 %collective-permute-done.1 = bf16[128,1024]{1,0:T(8,128)(2,1)S(1)} collective-permute-done((bf16[128,1024]{1,0:T(8,128)(2,1)S(1)}, bf16[128,1024]{1,0:T(8,128)(2,1)S(1)}, u32[]{:S(2)}, u32[]{:S(2)}) %collective-permute-start.1) | collective-permute-done | bytes 262176 | tf_op jit(solution)/shard_map/ppermute | solution.py:224
  11.4 0.1 fusion
  11.5 1.6 %collective-permute-start.6 = (bf16[32,1024]{1,0:T(8,128)(2,1)S(1)}, bf16[32,1024]{1,0:T(8,128)(2,1)S(1)}, u32[]{:S(2)}, u32[]{:S(2)}) collective-permute-start(bf16[32,1024]{1,0:T(8,128)(2,1)S(1)} %get-tuple-element.54), channel_id=1, source_target_pairs={{0,4},{1,5},{2,6},{3,7},{4,0},{5,1},{6,2},{7,3},{8,12},{9,13},{10,... | collective-permute-start | bytes 196616 | tf_op jit(solution)/shard_map/ppermute | solution.py:224
  13.1 1.5 %collective-permute-start.7 = (bf16[32,1024]{1,0:T(8,128)(2,1)S(1)}, bf16[32,1024]{1,0:T(8,128)(2,1)S(1)}, u32[]{:S(2)}, u32[]{:S(2)}) collective-permute-start(bf16[32,1024]{1,0:T(8,128)(2,1)S(1)} %get-tuple-element.54), channel_id=1, source_target_pairs={{0,2},{1,3},{2,0},{3,1},{4,6},{5,7},{6,4},{7,5},{8,10},{9,11},{10,... | collective-permute-start | bytes 196616 | tf_op jit(solution)/shard_map/ppermute | solution.py:224
  14.6 0.4 %collective-permute-start.8 = (bf16[32,1024]{1,0:T(8,128)(2,1)S(1)}, bf16[32,1024]{1,0:T(8,128)(2,1)S(1)}, u32[]{:S(2)}, u32[]{:S(2)}) collective-permute-start(bf16[32,1024]{1,0:T(8,128)(2,1)S(1)} %get-tuple-element.54), channel_id=1, source_target_pairs={{0,6},{1,7},{2,4},{3,5},{4,2},{5,3},{6,0},{7,1},{8,14},{9,15},{10,... | collective-permute-start | bytes 196616 | tf_op jit(solution)/shard_map/ppermute | solution.py:224
  15.1 2.6 %collective-permute-start.2 = (bf16[32,1024]{1,0:T(8,128)(2,1)S(1)}, bf16[32,1024]{1,0:T(8,128)(2,1)S(1)}, u32[]{:S(2)}, u32[]{:S(2)}) collective-permute-start(bf16[32,1024]{1,0:T(8,128)(2,1)S(1)} %get-tuple-element.51), channel_id=1, source_target_pairs={{0,6},{1,7},{2,4},{3,5},{4,2},{5,3},{6,0},{7,1},{8,14},{9,15},{10,... | collective-permute-start | bytes 196616 | tf_op jit(solution)/shard_map/ppermute | solution.py:224
  17.6 0.5 %collective-permute-start.3 = (bf16[32,1024]{1,0:T(8,128)(2,1)S(1)}, bf16[32,1024]{1,0:T(8,128)(2,1)S(1)}, u32[]{:S(2)}, u32[]{:S(2)}) collective-permute-start(bf16[32,1024]{1,0:T(8,128)(2,1)S(1)} %get-tuple-element.53), channel_id=1, source_target_pairs={{0,2},{1,3},{2,0},{3,1},{4,6},{5,7},{6,4},{7,5},{8,10},{9,11},{10,... | collective-permute-start | bytes 196616 | tf_op jit(solution)/shard_map/ppermute | solution.py:224
  18.1 0.0 collective-permute-done.6
  18.1 0.5 %collective-permute-start.4 = (bf16[32,1024]{1,0:T(8,128)(2,1)S(1)}, bf16[32,1024]{1,0:T(8,128)(2,1)S(1)}, u32[]{:S(2)}, u32[]{:S(2)}) collective-permute-start(bf16[32,1024]{1,0:T(8,128)(2,1)S(1)} %get-tuple-element.52), channel_id=1, source_target_pairs={{0,4},{1,5},{2,6},{3,7},{4,0},{5,1},{6,2},{7,3},{8,12},{9,13},{10,... | collective-permute-start | bytes 196616 | tf_op jit(solution)/shard_map/ppermute | solution.py:224
  18.6 1.2 %collective-permute-done.8 = bf16[32,1024]{1,0:T(8,128)(2,1)S(1)} collective-permute-done((bf16[32,1024]{1,0:T(8,128)(2,1)S(1)}, bf16[32,1024]{1,0:T(8,128)(2,1)S(1)}, u32[]{:S(2)}, u32[]{:S(2)}) %collective-permute-start.8) | collective-permute-done | bytes 65568 | tf_op jit(solution)/shard_map/ppermute | solution.py:224
  19.9 0.7 %collective-permute-done.2 = bf16[32,1024]{1,0:T(8,128)(2,1)S(1)} collective-permute-done((bf16[32,1024]{1,0:T(8,128)(2,1)S(1)}, bf16[32,1024]{1,0:T(8,128)(2,1)S(1)}, u32[]{:S(2)}, u32[]{:S(2)}) %collective-permute-start.2) | collective-permute-done | bytes 65568 | tf_op jit(solution)/shard_map/ppermute | solution.py:224
  20.6 1.3 %collective-permute-done.3 = bf16[32,1024]{1,0:T(8,128)(2,1)S(1)} collective-permute-done((bf16[32,1024]{1,0:T(8,128)(2,1)S(1)}, bf16[32,1024]{1,0:T(8,128)(2,1)S(1)}, u32[]{:S(2)}, u32[]{:S(2)}) %collective-permute-start.3) | collective-permute-done | bytes 65568 | tf_op jit(solution)/shard_map/ppermute | solution.py:224
  21.9 0.5 %collective-permute-done.4 = bf16[32,1024]{1,0:T(8,128)(2,1)S(1)} collective-permute-done((bf16[32,1024]{1,0:T(8,128)(2,1)S(1)}, bf16[32,1024]{1,0:T(8,128)(2,1)S(1)}, u32[]{:S(2)}, u32[]{:S(2)}) %collective-permute-start.4) | collective-permute-done | bytes 65568 | tf_op jit(solution)/shard_map/ppermute | solution.py:224
  22.5 2.9 %collective-permute-start.5 = (bf16[16,1024]{1,0:T(8,128)(2,1)S(1)}, bf16[16,1024]{1,0:T(8,128)(2,1)S(1)}, u32[]{:S(2)}, u32[]{:S(2)}) collective-permute-start(bf16[16,1024]{1,0:T(8,128)(2,1)S(1)} %slice.35), channel_id=1, source_target_pairs={{0,8},{1,9},{2,10},{3,11},{4,12},{5,13},{6,14},{7,15},{8,0},{9,1},... | collective-permute-start | bytes 98312 | tf_op jit(solution)/shard_map/ppermute | solution.py:224
  25.4 1.3 %outer.1.outer_ref = bf16[32,512,128]{2,1,0:T(8,128)(2,1)S(1)} custom-call(bf16[128,1024]{1,0:T(8,128)(2,1)S(1)} %constant_dynamic-update-slice_fusion.2.near_ref, bf16[128,1024]{1,0:T(8,128)(2,1)S(1)} %collective-permute-done.9.far_ref, bf16[256,2048]{1,0:T(8,128)(2,1)S(1)} %get-tuple-element.35.scaled_ref), custom_call_target="tpu_custom_call" | custom-call | flops 67108864 | bytes 1048576 | tf_op jit(solution)/shard_map/outer/pallas_call | solution.py:204
  26.7 1.5 %left.1.refs_2_ = f32[64,512]{1,0:T(8,128)S(1)} custom-call(bf16[32,512,128]{2,1,0:T(8,128)(2,1)S(1)} %outer.1.outer_ref, bf16[1024,128]{1,0:T(8,128)(2,1)S(1)} %get-tuple-element.44.owp_ref, bf16[32,64]{1,0:T(8,128)(2,1)S(1)} %get-tuple-element.45.lw_ref), custom_call_target="tpu_custom_call" | custom-call | flops 67108864 | bytes 1048576 | tf_op jit(solution)/shard_map/left/pallas_call | solution.py:204
  28.2 1.5 %final.1 = f32[512,64]{1,0:T(8,128)} custom-call(f32[16,1024]{1,0:T(8,128)S(1)} %slice.32.keep_ref, bf16[16,1024]{1,0:T(8,128)(2,1)S(1)} %collective-permute-done.5.refs_0_, bf16[32,64]{1,0:T(8,128)(2,1)S(1)} %get-tuple-element.41.refs_1_, f32[64,512]{1,0:T(8,128)S(1)} %left.1.refs_2_, f32[64,512]{1,0:T(8,128)S(1)} %get-tuple-element.46.refs_3_, ...), custom_call_target="tpu_custom_call" | custom-call | bytes 1048576 | tf_op jit(solution)/shard_map/final/pallas_call | solution.py:204
  (14 shorter events, 0.1 us)
Async XLA Ops:
  2.7 6.3 %collective-permute-start = (bf16[16,1024]{1,0:T(8,128)(2,1)S(1)}, bf16[16,1024]{1,0:T(8,128)(2,1)S(1)}, u32[]{:S(2)}, u32[]{:S(2)}) collective-permute-start(bf16[16,1024]{1,0:T(8,128)(2,1)S(1)} %get-tuple-element.42), channel_id=1, source_target_pairs={{0,8},{1,9},{2,10},{3,11},{4,12},{5,13},{6,14},{7,15},{8,0},{9,1},... | collective-permute-start | bytes 98312 | tf_op jit(solution)/shard_map/ppermute | solution.py:224
  9.8 1.6 %collective-permute-start.1 = (bf16[128,1024]{1,0:T(8,128)(2,1)S(1)}, bf16[128,1024]{1,0:T(8,128)(2,1)S(1)}, u32[]{:S(2)}, u32[]{:S(2)}) collective-permute-start(bf16[128,1024]{1,0:T(8,128)(2,1)S(1)} %send.1), channel_id=1, source_target_pairs={{0,1},{1,0},{2,3},{3,2},{4,5},{5,4},{6,7},{7,6},{8,9},{9,8},{10,11... | collective-permute-start | bytes 786440 | tf_op jit(solution)/shard_map/ppermute | solution.py:224
  11.5 6.7 %collective-permute-start.6 = (bf16[32,1024]{1,0:T(8,128)(2,1)S(1)}, bf16[32,1024]{1,0:T(8,128)(2,1)S(1)}, u32[]{:S(2)}, u32[]{:S(2)}) collective-permute-start(bf16[32,1024]{1,0:T(8,128)(2,1)S(1)} %get-tuple-element.54), channel_id=1, source_target_pairs={{0,4},{1,5},{2,6},{3,7},{4,0},{5,1},{6,2},{7,3},{8,12},{9,13},{10,... | collective-permute-start | bytes 196616 | tf_op jit(solution)/shard_map/ppermute | solution.py:224
  13.1 5.5 %collective-permute-start.7 = (bf16[32,1024]{1,0:T(8,128)(2,1)S(1)}, bf16[32,1024]{1,0:T(8,128)(2,1)S(1)}, u32[]{:S(2)}, u32[]{:S(2)}) collective-permute-start(bf16[32,1024]{1,0:T(8,128)(2,1)S(1)} %get-tuple-element.54), channel_id=1, source_target_pairs={{0,2},{1,3},{2,0},{3,1},{4,6},{5,7},{6,4},{7,5},{8,10},{9,11},{10,... | collective-permute-start | bytes 196616 | tf_op jit(solution)/shard_map/ppermute | solution.py:224
  14.6 5.2 %collective-permute-start.8 = (bf16[32,1024]{1,0:T(8,128)(2,1)S(1)}, bf16[32,1024]{1,0:T(8,128)(2,1)S(1)}, u32[]{:S(2)}, u32[]{:S(2)}) collective-permute-start(bf16[32,1024]{1,0:T(8,128)(2,1)S(1)} %get-tuple-element.54), channel_id=1, source_target_pairs={{0,6},{1,7},{2,4},{3,5},{4,2},{5,3},{6,0},{7,1},{8,14},{9,15},{10,... | collective-permute-start | bytes 196616 | tf_op jit(solution)/shard_map/ppermute | solution.py:224
  15.1 5.6 %collective-permute-start.2 = (bf16[32,1024]{1,0:T(8,128)(2,1)S(1)}, bf16[32,1024]{1,0:T(8,128)(2,1)S(1)}, u32[]{:S(2)}, u32[]{:S(2)}) collective-permute-start(bf16[32,1024]{1,0:T(8,128)(2,1)S(1)} %get-tuple-element.51), channel_id=1, source_target_pairs={{0,6},{1,7},{2,4},{3,5},{4,2},{5,3},{6,0},{7,1},{8,14},{9,15},{10,... | collective-permute-start | bytes 196616 | tf_op jit(solution)/shard_map/ppermute | solution.py:224
  17.6 4.3 %collective-permute-start.3 = (bf16[32,1024]{1,0:T(8,128)(2,1)S(1)}, bf16[32,1024]{1,0:T(8,128)(2,1)S(1)}, u32[]{:S(2)}, u32[]{:S(2)}) collective-permute-start(bf16[32,1024]{1,0:T(8,128)(2,1)S(1)} %get-tuple-element.53), channel_id=1, source_target_pairs={{0,2},{1,3},{2,0},{3,1},{4,6},{5,7},{6,4},{7,5},{8,10},{9,11},{10,... | collective-permute-start | bytes 196616 | tf_op jit(solution)/shard_map/ppermute | solution.py:224
  18.1 4.3 %collective-permute-start.4 = (bf16[32,1024]{1,0:T(8,128)(2,1)S(1)}, bf16[32,1024]{1,0:T(8,128)(2,1)S(1)}, u32[]{:S(2)}, u32[]{:S(2)}) collective-permute-start(bf16[32,1024]{1,0:T(8,128)(2,1)S(1)} %get-tuple-element.52), channel_id=1, source_target_pairs={{0,4},{1,5},{2,6},{3,7},{4,0},{5,1},{6,2},{7,3},{8,12},{9,13},{10,... | collective-permute-start | bytes 196616 | tf_op jit(solution)/shard_map/ppermute | solution.py:224
  19.9 5.5 %collective-permute-start.9 = (bf16[128,1024]{1,0:T(8,128)(2,1)S(1)}, bf16[128,1024]{1,0:T(8,128)(2,1)S(1)}, u32[]{:S(2)}, u32[]{:S(2)}) collective-permute-start(bf16[128,1024]{1,0:T(8,128)(2,1)S(1)} %constant_dynamic-update-slice_fusion.2.near_ref), channel_id=1, source_target_pairs={{0,1},{1,0},{2,3},{3,2},{4,5},{5,4},{6,7},{7,6},{8,9},{9,8},{10,11... | collective-permute-start | bytes 786440 | tf_op jit(solution)/shard_map/ppermute | solution.py:224
  22.5 5.8 %collective-permute-start.5 = (bf16[16,1024]{1,0:T(8,128)(2,1)S(1)}, bf16[16,1024]{1,0:T(8,128)(2,1)S(1)}, u32[]{:S(2)}, u32[]{:S(2)}) collective-permute-start(bf16[16,1024]{1,0:T(8,128)(2,1)S(1)} %slice.35), channel_id=1, source_target_pairs={{0,8},{1,9},{2,10},{3,11},{4,12},{5,13},{6,14},{7,15},{8,0},{9,1},... | collective-permute-start | bytes 98312 | tf_op jit(solution)/shard_map/ppermute | solution.py:224

commit v4 on v3

--- a/solution.py
+++ b/solution.py
@@ -251,7 +251,7 @@
         in_specs=[pl.BlockSpec(memory_space=pl.ANY)] * len(sources),
     )
     bits = [1 << t for t in range(size.bit_length() - 1)]
-    stages = [bits[:1]] + [bits[t : t + 2] for t in range(1, len(bits), 2)]
+    stages = [bits[t : t + 2] for t in range(1, len(bits), 2)]
 
     def partners(stage):
         found = [0]
@@ -259,19 +259,13 @@
             found = found + [bit ^ f for f in found]
         return found
 
-    def gather(blocks, stage):
-        block = jnp.concatenate(blocks, axis=0) if len(blocks) > 1 else blocks[0]
-        return [block] + [exchange(block, other) for other in partners(stage)[:0:-1]][::-1]
-
-    def scatter(total, stage):
-        others = partners(stage)
-        part = total.shape[0] // len(others)
-        got = [
-            exchange(total[t * part : (t + 1) * part].astype(BF16), others[t]) for t in range(len(others) - 1, 0, -1)
-        ]
-        return total[:part], got
-
-    blocks = gather([right], stages[-1])
+    def parts(total, stage):
+        return [piece.astype(BF16) for piece in jnp.split(total, 1 << len(stage))]
+
+    block = right
+    for stage in stages[:0:-1]:
+        block = [block] + [exchange(block, other) for other in partners(stage)[1:]]
+        block = jnp.concatenate(block, axis=0)
     scaled, spread = call(
         functools.partial(spread_kernel, rows, size),
         "spread",
@@ -279,7 +273,6 @@
         [near(v) for v in (g, inverse, left, stack)],
         flops=2 * 2**30,
     )
-    blocks, spread = lax.optimization_barrier((blocks, spread))
     send = call(
         send_kernel,
         "send",
@@ -287,6 +280,7 @@
         [near(scaled), near(spread)],
         flops=2**30,
     )
+    scaled_again, send, block = lax.optimization_barrier((scaled, send, block))
     got = exchange(send, bits[0])
     keep, normed, recip, presence = call(
         functools.partial(keep_kernel, rows),
@@ -297,18 +291,23 @@
             near_shape((1, count), F32),
             near_shape((1, count), F32),
         ),
-        [near(v) for v in (scaled, spread, x, mask)],
+        [near(v) for v in (scaled_again, spread, x, mask)],
         flops=2**30,
     )
-    got = [got]
-    for number, stage in enumerate(stages[1:], 1):
-        for piece in got:
-            keep = keep + piece.astype(F32)
-        keep, got = scatter(keep, stage)
-        if number < len(stages) - 1:
-            blocks, keep = lax.optimization_barrier((blocks, keep))
-            blocks = gather(blocks, stages[-1 - number])
-    near_block, far_block = gather(blocks, stages[0])
+    total = keep + got.astype(F32)
+    sums = parts(total, stages[0])
+    joint = [
+        exchange(jnp.concatenate([piece, block], axis=0), other) for piece, other in zip(sums[1:], partners(stages[0])[1:])
+    ]
+    cut = sums[0].shape[0]
+    near_block = jnp.concatenate([block] + [v[cut:] for v in joint], axis=0)
+    far_block = exchange(near_block, bits[0])
+    keep, got = total[:cut], [v[:cut] for v in joint]
+    for stage in stages[1:]:
+        total = keep + sum(v.astype(F32) for v in got)
+        sums = parts(total, stage)
+        keep = total[: sums[0].shape[0]]
+        got = [exchange(piece, other) for piece, other in zip(sums[1:], partners(stage)[1:])]
     outer = call(
         functools.partial(outer_kernel, rows),
         "outer",

time: 29.9 us -> 28 us (0.936)
  starting transfers between devices: 14.2 us -> 10.6 us
  waiting for transfers between devices: 5.2 us -> 6.83 us
    ppermute x10 -> x7, starting transfers between devices: 14.2 us -> 10.6 us  [exchange(): return lax.ppermute(value, 'row', [(d, d ^ bit) for d in range(size)])]
    ppermute x10 -> x7, waiting for transfers between devices: 5.2 us -> 6.83 us  [exchange(): return lax.ppermute(value, 'row', [(d, d ^ bit) for d in range(size)])]
  transfers between devices with their start and end apart: 10 -> 7, of which waited for: 6 -> 4; matrix products, arithmetic and copies ran while one was open for 0% -> 0% of each run, Pallas kernels for 17% -> 19%
where the time goes in v4:
time: 28 us; the launch traced here: 27.8 us
  starting transfers between devices  10.6 us (38%)
  Pallas kernels  10.1 us (36%)
  waiting for transfers between devices  6.83 us (24%)
    ppermute x7, starting transfers between devices, exchange(): return lax.ppermute(value, 'row', [(d, d ^ bit) for d in range(size)])  10.6 us
    pallas_call x7, Pallas kernels, call(): pl.pallas_call(kernel, out_shape=out_shape, in_specs=in_specs or [vmem] *...  10.1 us
    ppermute x7, waiting for transfers between devices, exchange(): return lax.ppermute(value, 'row', [(d, d ^ bit) for d in range(size)])  6.83 us
  transfers between devices with their start and end apart: 7, of which 4 were waited for; matrix products, arithmetic and copies ran while one was open for 0% of the time, Pallas kernels for 19%

profile of v4, /device:TPU:0, one launch (start us, length us, event | category | flops | bytes accessed | tf_op | source)
XLA Modules:
  0.0 27.8 jit_solution(17280845697835308141)
XLA Ops:
  0.0 2.6 %project.1 = (bf16[32,512]{1,0:T(8,128)(2,1)S(1)}, bf16[16,1024]{1,0:T(8,128)(2,1)S(1)}, bf16[512,64]{1,0:T(8,128)(2,1)S(1)}, s32[32,256]{1,0:T(8,128)S(1)}, bf1...) custom-call(bf16[512,64]{1,0:T(8,128)(2,1)} %bitcast.5, ...), custom_call_target="tpu_custom_call" | custom-call | bytes 1048576 | tf_op jit(solution)/shard_map/project/pallas_call | solution.py:204
  2.7 4.1 %collective-permute-start = (bf16[16,1024]{1,0:T(8,128)(2,1)S(1)}, bf16[16,1024]{1,0:T(8,128)(2,1)S(1)}, u32[]{:S(2)}, u32[]{:S(2)}) collective-permute-start(bf16[16,1024]{1,0:T(8,128)(2,1)S(1)} %get-tuple-element.30), channel_id=1, source_target_pairs={{0,8},{1,9},{2,10},{3,11},{4,12},{5,13},{6,14},{7,15},{8,0},{9,1},... | collective-permute-start | bytes 98312 | tf_op jit(solution)/shard_map/ppermute | solution.py:224
  6.8 1.4 %spread.1 = (bf16[256,2048]{1,0:T(8,128)(2,1)S(1)}, bf16[2048,1024]{1,0:T(8,128)(2,1)S(1)}) custom-call(bf16[16,256,128]{2,1,0:T(8,128)(2,1)S(1)} %get-tuple-element.24.g_ref, f32[256,16]{1,0:T(8,128)S(1)} %get-tuple-element.25.inverse_ref, bf16[32,512]{1,0:T(8,128)(2,1)S(1)} %get-tuple-element.26.left_ref, bf16[512,256]{1,0:T(8,128)(2,1)S(1)} %get-tuple-element.27.stack_ref), custom_call_target="tpu_custom_call" | custom-call | flops 2147483648 | bytes 1048576 | tf_op jit(solution)/shard_map/spread/pallas_call | solution.py:204
  8.2 0.7 %send.1 = bf16[128,1024]{1,0:T(8,128)(2,1)S(1)} custom-call(bf16[256,2048]{1,0:T(8,128)(2,1)S(1)} %get-tuple-element.31.scaled_ref, bf16[2048,1024]{1,0:T(8,128)(2,1)S(1)} %get-tuple-element.29.spread_ref), custom_call_target="tpu_custom_call" | custom-call | flops 1073741824 | bytes 1048576 | tf_op jit(solution)/shard_map/send/pallas_call | solution.py:204
  8.9 0.1 collective-permute-done
  9.0 0.0 collective-permute-start.1
  9.1 0.9 %keep.1 = (f32[128,1024]{1,0:T(8,128)S(1)}, f32[64,512]{1,0:T(8,128)S(1)}, f32[1,512]{1,0:T(1,128)S(1)}, f32[1,512]{1,0:T(1,128)S(1)}) custom-call(bf16[256,2048]{1,0:T(8,128)(2,1)S(1)} %get-tuple-element.31.scaled_ref, bf16[2048,1024]{1,0:T(8,128)(2,1)S(1)} %get-tuple-element.29.spread_ref, bf16[512,64]{1,0:T(8,128)(2,1)S(1)} %get-tuple-element.32.x_ref, ...), custom_call_target="tpu_custom_call" | custom-call | flops 1073741824 | bytes 1048576 | tf_op jit(solution)/shard_map/keep/pallas_call | solution.py:204
  10.0 0.6 %collective-permute-done.1 = bf16[128,1024]{1,0:T(8,128)(2,1)S(1)} collective-permute-done((bf16[128,1024]{1,0:T(8,128)(2,1)S(1)}, bf16[128,1024]{1,0:T(8,128)(2,1)S(1)}, u32[]{:S(2)}, u32[]{:S(2)}) %collective-permute-start.1) | collective-permute-done | bytes 262176 | tf_op jit(solution)/shard_map/ppermute | solution.py:224
  10.6 0.1 fusion
  10.7 1.6 %collective-permute-start.2 = (bf16[64,1024]{1,0:T(8,128)(2,1)S(1)}, bf16[64,1024]{1,0:T(8,128)(2,1)S(1)}, u32[]{:S(2)}, u32[]{:S(2)}) collective-permute-start(bf16[64,1024]{1,0:T(8,128)(2,1)S(1)} %get-tuple-element.48), channel_id=1, source_target_pairs={{0,4},{1,5},{2,6},{3,7},{4,0},{5,1},{6,2},{7,3},{8,12},{9,13},{10,... | collective-permute-start | bytes 393224 | tf_op jit(solution)/shard_map/ppermute | solution.py:224
  12.4 1.5 %collective-permute-start.3 = (bf16[64,1024]{1,0:T(8,128)(2,1)S(1)}, bf16[64,1024]{1,0:T(8,128)(2,1)S(1)}, u32[]{:S(2)}, u32[]{:S(2)}) collective-permute-start(bf16[64,1024]{1,0:T(8,128)(2,1)S(1)} %get-tuple-element.49), channel_id=1, source_target_pairs={{0,2},{1,3},{2,0},{3,1},{4,6},{5,7},{6,4},{7,5},{8,10},{9,11},{10,... | collective-permute-start | bytes 393224 | tf_op jit(solution)/shard_map/ppermute | solution.py:224
  13.9 0.4 %collective-permute-start.4 = (bf16[64,1024]{1,0:T(8,128)(2,1)S(1)}, bf16[64,1024]{1,0:T(8,128)(2,1)S(1)}, u32[]{:S(2)}, u32[]{:S(2)}) collective-permute-start(bf16[64,1024]{1,0:T(8,128)(2,1)S(1)} %get-tuple-element.50), channel_id=1, source_target_pairs={{0,6},{1,7},{2,4},{3,5},{4,2},{5,3},{6,0},{7,1},{8,14},{9,15},{10,... | collective-permute-start | bytes 393224 | tf_op jit(solution)/shard_map/ppermute | solution.py:224
  14.3 2.3 %collective-permute-done.2 = bf16[64,1024]{1,0:T(8,128)(2,1)S(1)} collective-permute-done((bf16[64,1024]{1,0:T(8,128)(2,1)S(1)}, bf16[64,1024]{1,0:T(8,128)(2,1)S(1)}, u32[]{:S(2)}, u32[]{:S(2)}) %collective-permute-start.2) | collective-permute-done | bytes 131104 | tf_op jit(solution)/shard_map/ppermute | solution.py:224
  16.6 3.8 %collective-permute-done.3 = bf16[64,1024]{1,0:T(8,128)(2,1)S(1)} collective-permute-done((bf16[64,1024]{1,0:T(8,128)(2,1)S(1)}, bf16[64,1024]{1,0:T(8,128)(2,1)S(1)}, u32[]{:S(2)}, u32[]{:S(2)}) %collective-permute-start.3) | collective-permute-done | bytes 131104 | tf_op jit(solution)/shard_map/ppermute | solution.py:224
  20.4 0.0 collective-permute-done.4
  20.5 0.1 collective-permute-start.6
  20.6 2.8 %collective-permute-start.5 = (bf16[16,1024]{1,0:T(8,128)(2,1)S(1)}, bf16[16,1024]{1,0:T(8,128)(2,1)S(1)}, u32[]{:S(2)}, u32[]{:S(2)}) collective-permute-start(bf16[16,1024]{1,0:T(8,128)(2,1)S(1)} %split.25), channel_id=1, source_target_pairs={{0,8},{1,9},{2,10},{3,11},{4,12},{5,13},{6,14},{7,15},{8,0},{9,1},... | collective-permute-start | bytes 98312 | tf_op jit(solution)/shard_map/ppermute | solution.py:224
  23.5 0.0 collective-permute-done.6.far_ref
  23.5 1.3 %outer.1.outer_ref = bf16[32,512,128]{2,1,0:T(8,128)(2,1)S(1)} custom-call(bf16[128,1024]{1,0:T(8,128)(2,1)S(1)} %pad_maximum_fusion.near_ref, bf16[128,1024]{1,0:T(8,128)(2,1)S(1)} %collective-permute-done.6.far_ref, bf16[256,2048]{1,0:T(8,128)(2,1)S(1)} %get-tuple-element.31.scaled_ref), custom_call_target="tpu_custom_call" | custom-call | flops 67108864 | bytes 1048576 | tf_op jit(solution)/shard_map/outer/pallas_call | solution.py:204
  24.8 1.5 %left.1.refs_2_ = f32[64,512]{1,0:T(8,128)S(1)} custom-call(bf16[32,512,128]{2,1,0:T(8,128)(2,1)S(1)} %outer.1.outer_ref, bf16[1024,128]{1,0:T(8,128)(2,1)S(1)} %get-tuple-element.38.owp_ref, bf16[32,64]{1,0:T(8,128)(2,1)S(1)} %get-tuple-element.39.lw_ref), custom_call_target="tpu_custom_call" | custom-call | flops 67108864 | bytes 1048576 | tf_op jit(solution)/shard_map/left/pallas_call | solution.py:204
  26.3 0.0 collective-permute-done.5.refs_0_
  26.3 1.5 %final.1 = f32[512,64]{1,0:T(8,128)} custom-call(f32[16,1024]{1,0:T(8,128)S(1)} %slice.36.keep_ref, bf16[16,1024]{1,0:T(8,128)(2,1)S(1)} %collective-permute-done.5.refs_0_, bf16[32,64]{1,0:T(8,128)(2,1)S(1)} %get-tuple-element.37.refs_1_, f32[64,512]{1,0:T(8,128)S(1)} %left.1.refs_2_, f32[64,512]{1,0:T(8,128)S(1)} %get-tuple-element.40.refs_3_, ...), custom_call_target="tpu_custom_call" | custom-call | bytes 1048576 | tf_op jit(solution)/shard_map/final/pallas_call | solution.py:204
  (10 shorter events, 0.1 us)
Async XLA Ops:
  2.7 6.3 %collective-permute-start = (bf16[16,1024]{1,0:T(8,128)(2,1)S(1)}, bf16[16,1024]{1,0:T(8,128)(2,1)S(1)}, u32[]{:S(2)}, u32[]{:S(2)}) collective-permute-start(bf16[16,1024]{1,0:T(8,128)(2,1)S(1)} %get-tuple-element.30), channel_id=1, source_target_pairs={{0,8},{1,9},{2,10},{3,11},{4,12},{5,13},{6,14},{7,15},{8,0},{9,1},... | collective-permute-start | bytes 98312 | tf_op jit(solution)/shard_map/ppermute | solution.py:224
  9.0 1.6 %collective-permute-start.1 = (bf16[128,1024]{1,0:T(8,128)(2,1)S(1)}, bf16[128,1024]{1,0:T(8,128)(2,1)S(1)}, u32[]{:S(2)}, u32[]{:S(2)}) collective-permute-start(bf16[128,1024]{1,0:T(8,128)(2,1)S(1)} %send.1), channel_id=1, source_target_pairs={{0,1},{1,0},{2,3},{3,2},{4,5},{5,4},{6,7},{7,6},{8,9},{9,8},{10,11... | collective-permute-start | bytes 786440 | tf_op jit(solution)/shard_map/ppermute | solution.py:224
  10.7 5.9 %collective-permute-start.2 = (bf16[64,1024]{1,0:T(8,128)(2,1)S(1)}, bf16[64,1024]{1,0:T(8,128)(2,1)S(1)}, u32[]{:S(2)}, u32[]{:S(2)}) collective-permute-start(bf16[64,1024]{1,0:T(8,128)(2,1)S(1)} %get-tuple-element.48), channel_id=1, source_target_pairs={{0,4},{1,5},{2,6},{3,7},{4,0},{5,1},{6,2},{7,3},{8,12},{9,13},{10,... | collective-permute-start | bytes 393224 | tf_op jit(solution)/shard_map/ppermute | solution.py:224
  12.4 8.1 %collective-permute-start.3 = (bf16[64,1024]{1,0:T(8,128)(2,1)S(1)}, bf16[64,1024]{1,0:T(8,128)(2,1)S(1)}, u32[]{:S(2)}, u32[]{:S(2)}) collective-permute-start(bf16[64,1024]{1,0:T(8,128)(2,1)S(1)} %get-tuple-element.49), channel_id=1, source_target_pairs={{0,2},{1,3},{2,0},{3,1},{4,6},{5,7},{6,4},{7,5},{8,10},{9,11},{10,... | collective-permute-start | bytes 393224 | tf_op jit(solution)/shard_map/ppermute | solution.py:224
  13.9 6.6 %collective-permute-start.4 = (bf16[64,1024]{1,0:T(8,128)(2,1)S(1)}, bf16[64,1024]{1,0:T(8,128)(2,1)S(1)}, u32[]{:S(2)}, u32[]{:S(2)}) collective-permute-start(bf16[64,1024]{1,0:T(8,128)(2,1)S(1)} %get-tuple-element.50), channel_id=1, source_target_pairs={{0,6},{1,7},{2,4},{3,5},{4,2},{5,3},{6,0},{7,1},{8,14},{9,15},{10,... | collective-permute-start | bytes 393224 | tf_op jit(solution)/shard_map/ppermute | solution.py:224
  20.5 3.0 %collective-permute-start.6 = (bf16[128,1024]{1,0:T(8,128)(2,1)S(1)}, bf16[128,1024]{1,0:T(8,128)(2,1)S(1)}, u32[]{:S(2)}, u32[]{:S(2)}) collective-permute-start(bf16[128,1024]{1,0:T(8,128)(2,1)S(1)} %pad_maximum_fusion.near_ref), channel_id=1, source_target_pairs={{0,1},{1,0},{2,3},{3,2},{4,5},{5,4},{6,7},{7,6},{8,9},{9,8},{10,11... | collective-permute-start | bytes 786440 | tf_op jit(solution)/shard_map/ppermute | solution.py:224
  20.6 5.7 %collective-permute-start.5 = (bf16[16,1024]{1,0:T(8,128)(2,1)S(1)}, bf16[16,1024]{1,0:T(8,128)(2,1)S(1)}, u32[]{:S(2)}, u32[]{:S(2)}) collective-permute-start(bf16[16,1024]{1,0:T(8,128)(2,1)S(1)} %split.25), channel_id=1, source_target_pairs={{0,8},{1,9},{2,10},{3,11},{4,12},{5,13},{6,14},{7,15},{8,0},{9,1},... | collective-permute-start | bytes 98312 | tf_op jit(solution)/shard_map/ppermute | solution.py:224

commit v5 on v4

--- a/solution.py
+++ b/solution.py
@@ -22,16 +22,19 @@
     return jnp.dot(mask.astype(F32).astype(BF16), pick.astype(F32).astype(BF16), preferred_element_type=F32)
 
 
-def presence_row(own, sequence_major):
+def presence_row(own):
     depth, rows = own.shape
     count = depth * rows
-    column = iota((rows, count), 1)
-    residue = column % rows if sequence_major else column // depth
-    spread = (residue == iota((rows, count), 0)).astype(F32).astype(BF16)
+    spread = (iota((rows, count), 1) // depth == iota((rows, count), 0)).astype(F32).astype(BF16)
     wide = jnp.dot(own.astype(BF16), spread, preferred_element_type=F32)
-    column = iota((depth, count), 1)
-    sequence = column // rows if sequence_major else column % depth
-    return jnp.sum(jnp.where(sequence == iota((depth, count), 0), wide, 0.0), axis=0, keepdims=True)
+    return jnp.sum(
+        jnp.where(iota((depth, count), 1) % depth == iota((depth, count), 0), wide, 0.0), axis=0, keepdims=True
+    )
+
+
+def by_residue(wide_ref, rows):
+    depth = wide_ref.shape[0] // rows
+    return jnp.concatenate([wide_ref[pl.ds(i, depth, stride=rows), :] for i in range(rows)], axis=0)
 
 
 def project_kernel(
@@ -58,16 +61,15 @@
     value = centered * recip
     normed[...] = value
     own = own_presence(mask_ref[...], me, rows)
-    right = lax.dot_general(rw_ref[...], value.astype(BF16), NT, preferred_element_type=F32)
-    right = right * presence_row(own, True)
-    for s in range(depth):
-        flat[pl.ds(s, hidden, stride=depth), :] = right[:, s * rows : (s + 1) * rows]
-    right_ref[...] = flat[...].T.astype(BF16)
-    by_residue = jnp.concatenate(
-        [normed[pl.ds(i, depth, stride=rows), :] for i in range(rows)], axis=0
+    weights = jnp.concatenate([lw_ref[...], rw_ref[...]], axis=0)
+    both = lax.dot_general(weights, by_residue(normed, rows).astype(BF16), NT, preferred_element_type=F32)
+    both = both * presence_row(own)
+    left_ref[...] = both[:hidden].astype(BF16)
+    for j in range(rows):
+        flat[j * hidden : (j + 1) * hidden, :] = both[hidden:, j * depth : (j + 1) * depth]
+    right_ref[...] = jnp.concatenate(
+        [flat[pl.ds(e, rows, stride=hidden), :] for e in range(hidden)], axis=1
     ).astype(BF16)
-    left = lax.dot_general(lw_ref[...], by_residue, NT, preferred_element_type=F32)
-    left_ref[...] = (left * presence_row(own, False)).astype(BF16)
     mask = mask_ref[...].astype(F32)
     residue = res_ref[...].astype(F32)
     residue_own = own_presence(jnp.broadcast_to(res_ref[...], (8, width)), me, rows)[:1]
@@ -118,15 +120,18 @@
     send_ref[...] = jnp.dot(scaled_ref[half:, :], spread_ref[...], preferred_element_type=F32).astype(BF16)
 
 
-def keep_kernel(rows, scaled_ref, spread_ref, x_ref, mask_ref, keep_ref, normed_ref, recip_ref, presence_ref):
+def keep_kernel(
+    rows, scaled_ref, spread_ref, x_ref, mask_ref, keep_ref, normed_ref, recip_ref, presence_ref, wide
+):
     half = keep_ref.shape[0]
     keep_ref[...] = jnp.dot(scaled_ref[:half, :], spread_ref[...], preferred_element_type=F32)
-    value = x_ref[...].astype(F32).T
+    wide[...] = x_ref[...].astype(F32)
+    value = by_residue(wide, rows).T
     centered = value - jnp.mean(value, axis=0, keepdims=True)
     recip = lax.rsqrt(jnp.mean(centered * centered, axis=0, keepdims=True) + 1e-05)
     normed_ref[...] = centered * recip
     recip_ref[...] = recip
-    presence_ref[...] = presence_row(own_presence(mask_ref[...], lax.axis_index("row"), rows), True)
+    presence_ref[...] = presence_row(own_presence(mask_ref[...], lax.axis_index("row"), rows))
 
 
 def weigh(weight, value):
@@ -153,10 +158,8 @@
             outer_ref[:, i * depth : (i + 1) * depth, :] = out[:, h * pair : (h + 1) * pair].reshape(hidden, depth, pair)
 
 
-def left_kernel(rows, outer_ref, owp_ref, lw_ref, grad_ref, total):
-    hidden = lw_ref.shape[0]
-    count = total.shape[0]
-    depth = count // rows
+def left_kernel(outer_ref, owp_ref, lw_ref, grad_ref):
+    hidden, count, _ = outer_ref.shape
     acc = jnp.zeros((count, hidden), F32)
     for e in range(0, hidden, 2):
         lhs = jnp.concatenate([outer_ref[e], outer_ref[e + 1]], axis=1)
@@ -164,26 +167,26 @@
             [owp_ref[e * hidden : (e + 1) * hidden, :], owp_ref[(e + 1) * hidden : (e + 2) * hidden, :]], axis=1
         )
         acc = acc + lax.dot_general(lhs, rhs, NT, preferred_element_type=F32)
-    total[...] = acc
-    by_sequence = jnp.concatenate([total[pl.ds(s, rows, stride=depth), :] for s in range(depth)], axis=0)
-    grad_ref[...] = weigh(lw_ref[...], by_sequence.T)
+    grad_ref[...] = weigh(lw_ref[...], acc.T)
 
 
 def final_kernel(rows, keep_ref, *refs):
-    *got_refs, rw_ref, grad_ref, normed_ref, recip_ref, presence_ref, out_ref, flat, lanes = refs
+    *got_refs, rw_ref, grad_ref, normed_ref, recip_ref, presence_ref, out_ref, flat = refs
     hidden = rw_ref.shape[0]
     depth = keep_ref.shape[1] // hidden
     total = keep_ref[...]
     for got_ref in got_refs:
         total = total + got_ref[...].astype(F32)
-    flat[...] = total.T
-    for s in range(depth):
-        lanes[:, s * rows : (s + 1) * rows] = flat[pl.ds(s, hidden, stride=depth), :]
-    grad = (weigh(rw_ref[...], lanes[...]) + grad_ref[...]) * presence_ref[...]
+    for e in range(hidden):
+        flat[pl.ds(e, rows, stride=hidden), :] = total[:, e * depth : (e + 1) * depth]
+    right = jnp.concatenate([flat[j * hidden : (j + 1) * hidden, :] for j in range(rows)], axis=1)
+    grad = (weigh(rw_ref[...], right) + grad_ref[...]) * presence_ref[...]
     normed = normed_ref[...]
     mean = jnp.mean(grad, axis=0, keepdims=True)
     cross = jnp.mean(grad * normed, axis=0, keepdims=True)
-    out_ref[...] = (recip_ref[...] * (grad - mean - normed * cross)).T
+    out = (recip_ref[...] * (grad - mean - normed * cross)).T
+    for i in range(rows):
+        out_ref[pl.ds(i, depth, stride=rows), :] = out[i * depth : (i + 1) * depth, :]
 
 
 def near_shape(dims, dtype):
@@ -244,7 +247,7 @@
             pltpu.VMEM((1, width), residue_mask.dtype),
             pltpu.VMEM(ow.shape, BF16),
             pltpu.VMEM((count, channels), F32),
-            pltpu.VMEM((flat_width, rows), F32),
+            pltpu.VMEM((rows * hidden, depth), F32),
             pltpu.VMEM(ow.shape, F32),
             pltpu.SemaphoreType.DMA((len(sources),)),
         ],
@@ -292,6 +295,7 @@
             near_shape((1, count), F32),
         ),
         [near(v) for v in (scaled_again, spread, x, mask)],
+        [pltpu.VMEM((count, channels), F32)],
         flops=2**30,
     )
     total = keep + got.astype(F32)
@@ -317,11 +321,10 @@
         flops=2**26,
     )
     grad = call(
-        functools.partial(left_kernel, rows),
+        left_kernel,
         "left",
         near_shape((channels, count), F32),
         [near(v) for v in (outer, owp, lw)],
-        [pltpu.VMEM((count, hidden), F32)],
         flops=2**26,
     )
     out = call(
@@ -329,7 +332,7 @@
         "final",
         jax.ShapeDtypeStruct((count, channels), F32),
         [near(v) for v in (keep, *got, rw, grad, normed, recip, presence)],
-        [pltpu.VMEM((flat_width, rows), F32), pltpu.VMEM((hidden, count), F32)],
+        [pltpu.VMEM((rows * hidden, depth), F32)],
     )
     return out.reshape(depth, rows, channels)
 

time: 28 us -> 27.2 us (0.971)
  Pallas kernels: 10.1 us -> 9.32 us
    pallas_call x7, Pallas kernels: 10.1 us -> 9.32 us  [call(): pl.pallas_call(kernel, out_shape=out_shape, in_specs=in_specs or [vmem] *...]
where the time goes in v5:
time: 27.2 us; the launch traced here: 27.1 us
  starting transfers between devices  10.6 us (39%)
  Pallas kernels  9.32 us (34%)
  waiting for transfers between devices  6.83 us (25%)
    ppermute x7, starting transfers between devices, exchange(): return lax.ppermute(value, 'row', [(d, d ^ bit) for d in range(size)])  10.6 us
    pallas_call x7, Pallas kernels, call(): pl.pallas_call(kernel, out_shape=out_shape, in_specs=in_specs or [vmem] *...  9.32 us
    ppermute x7, waiting for transfers between devices, exchange(): return lax.ppermute(value, 'row', [(d, d ^ bit) for d in range(size)])  6.83 us
  transfers between devices with their start and end apart: 7, of which 4 were waited for; matrix products, arithmetic and copies ran while one was open for 0% of the time, Pallas kernels for 19%

profile of v5, /device:TPU:0, one launch (start us, length us, event | category | flops | bytes accessed | tf_op | source)
XLA Modules:
  0.0 27.1 jit_solution(3210648429598487835)
XLA Ops:
  0.0 2.2 %project.1 = (bf16[32,512]{1,0:T(8,128)(2,1)S(1)}, bf16[16,1024]{1,0:T(8,128)(2,1)S(1)}, bf16[512,64]{1,0:T(8,128)(2,1)S(1)}, s32[32,256]{1,0:T(8,128)S(1)}, bf1...) custom-call(bf16[512,64]{1,0:T(8,128)(2,1)} %bitcast.5, ...), custom_call_target="tpu_custom_call" | custom-call | bytes 1048576 | tf_op jit(solution)/shard_map/project/pallas_call | solution.py:207
  2.2 4.1 %collective-permute-start = (bf16[16,1024]{1,0:T(8,128)(2,1)S(1)}, bf16[16,1024]{1,0:T(8,128)(2,1)S(1)}, u32[]{:S(2)}, u32[]{:S(2)}) collective-permute-start(bf16[16,1024]{1,0:T(8,128)(2,1)S(1)} %get-tuple-element.30), channel_id=1, source_target_pairs={{0,8},{1,9},{2,10},{3,11},{4,12},{5,13},{6,14},{7,15},{8,0},{9,1},... | collective-permute-start | bytes 98312 | tf_op jit(solution)/shard_map/ppermute | solution.py:227
  6.3 1.4 %spread.1 = (bf16[256,2048]{1,0:T(8,128)(2,1)S(1)}, bf16[2048,1024]{1,0:T(8,128)(2,1)S(1)}) custom-call(bf16[16,256,128]{2,1,0:T(8,128)(2,1)S(1)} %get-tuple-element.24.g_ref, f32[256,16]{1,0:T(8,128)S(1)} %get-tuple-element.25.inverse_ref, bf16[32,512]{1,0:T(8,128)(2,1)S(1)} %get-tuple-element.26.left_ref, bf16[512,256]{1,0:T(8,128)(2,1)S(1)} %get-tuple-element.27.stack_ref), custom_call_target="tpu_custom_call" | custom-call | flops 2147483648 | bytes 1048576 | tf_op jit(solution)/shard_map/spread/pallas_call | solution.py:207
  7.7 0.7 %send.1 = bf16[128,1024]{1,0:T(8,128)(2,1)S(1)} custom-call(bf16[256,2048]{1,0:T(8,128)(2,1)S(1)} %get-tuple-element.31.scaled_ref, bf16[2048,1024]{1,0:T(8,128)(2,1)S(1)} %get-tuple-element.29.spread_ref), custom_call_target="tpu_custom_call" | custom-call | flops 1073741824 | bytes 1048576 | tf_op jit(solution)/shard_map/send/pallas_call | solution.py:207
  8.5 0.1 collective-permute-done
  8.5 0.0 collective-permute-start.1
  8.6 0.9 %keep.1 = (f32[128,1024]{1,0:T(8,128)S(1)}, f32[64,512]{1,0:T(8,128)S(1)}, f32[1,512]{1,0:T(1,128)S(1)}, f32[1,512]{1,0:T(1,128)S(1)}) custom-call(bf16[256,2048]{1,0:T(8,128)(2,1)S(1)} %get-tuple-element.31.scaled_ref, bf16[2048,1024]{1,0:T(8,128)(2,1)S(1)} %get-tuple-element.29.spread_ref, bf16[512,64]{1,0:T(8,128)(2,1)S(1)} %get-tuple-element.32.x_ref, ...), custom_call_target="tpu_custom_call" | custom-call | flops 1073741824 | bytes 1048576 | tf_op jit(solution)/shard_map/keep/pallas_call | solution.py:207
  9.5 0.6 %collective-permute-done.1 = bf16[128,1024]{1,0:T(8,128)(2,1)S(1)} collective-permute-done((bf16[128,1024]{1,0:T(8,128)(2,1)S(1)}, bf16[128,1024]{1,0:T(8,128)(2,1)S(1)}, u32[]{:S(2)}, u32[]{:S(2)}) %collective-permute-start.1) | collective-permute-done | bytes 262176 | tf_op jit(solution)/shard_map/ppermute | solution.py:227
  10.1 0.1 fusion
  10.3 1.6 %collective-permute-start.2 = (bf16[64,1024]{1,0:T(8,128)(2,1)S(1)}, bf16[64,1024]{1,0:T(8,128)(2,1)S(1)}, u32[]{:S(2)}, u32[]{:S(2)}) collective-permute-start(bf16[64,1024]{1,0:T(8,128)(2,1)S(1)} %get-tuple-element.48), channel_id=1, source_target_pairs={{0,4},{1,5},{2,6},{3,7},{4,0},{5,1},{6,2},{7,3},{8,12},{9,13},{10,... | collective-permute-start | bytes 393224 | tf_op jit(solution)/shard_map/ppermute | solution.py:227
  11.9 1.5 %collective-permute-start.3 = (bf16[64,1024]{1,0:T(8,128)(2,1)S(1)}, bf16[64,1024]{1,0:T(8,128)(2,1)S(1)}, u32[]{:S(2)}, u32[]{:S(2)}) collective-permute-start(bf16[64,1024]{1,0:T(8,128)(2,1)S(1)} %get-tuple-element.49), channel_id=1, source_target_pairs={{0,2},{1,3},{2,0},{3,1},{4,6},{5,7},{6,4},{7,5},{8,10},{9,11},{10,... | collective-permute-start | bytes 393224 | tf_op jit(solution)/shard_map/ppermute | solution.py:227
  13.4 0.4 %collective-permute-start.4 = (bf16[64,1024]{1,0:T(8,128)(2,1)S(1)}, bf16[64,1024]{1,0:T(8,128)(2,1)S(1)}, u32[]{:S(2)}, u32[]{:S(2)}) collective-permute-start(bf16[64,1024]{1,0:T(8,128)(2,1)S(1)} %get-tuple-element.50), channel_id=1, source_target_pairs={{0,6},{1,7},{2,4},{3,5},{4,2},{5,3},{6,0},{7,1},{8,14},{9,15},{10,... | collective-permute-start | bytes 393224 | tf_op jit(solution)/shard_map/ppermute | solution.py:227
  13.8 2.3 %collective-permute-done.2 = bf16[64,1024]{1,0:T(8,128)(2,1)S(1)} collective-permute-done((bf16[64,1024]{1,0:T(8,128)(2,1)S(1)}, bf16[64,1024]{1,0:T(8,128)(2,1)S(1)}, u32[]{:S(2)}, u32[]{:S(2)}) %collective-permute-start.2) | collective-permute-done | bytes 131104 | tf_op jit(solution)/shard_map/ppermute | solution.py:227
  16.1 3.8 %collective-permute-done.3 = bf16[64,1024]{1,0:T(8,128)(2,1)S(1)} collective-permute-done((bf16[64,1024]{1,0:T(8,128)(2,1)S(1)}, bf16[64,1024]{1,0:T(8,128)(2,1)S(1)}, u32[]{:S(2)}, u32[]{:S(2)}) %collective-permute-start.3) | collective-permute-done | bytes 131104 | tf_op jit(solution)/shard_map/ppermute | solution.py:227
  20.0 0.0 collective-permute-done.4
  20.0 0.1 collective-permute-start.6
  20.1 2.8 %collective-permute-start.5 = (bf16[16,1024]{1,0:T(8,128)(2,1)S(1)}, bf16[16,1024]{1,0:T(8,128)(2,1)S(1)}, u32[]{:S(2)}, u32[]{:S(2)}) collective-permute-start(bf16[16,1024]{1,0:T(8,128)(2,1)S(1)} %split.25), channel_id=1, source_target_pairs={{0,8},{1,9},{2,10},{3,11},{4,12},{5,13},{6,14},{7,15},{8,0},{9,1},... | collective-permute-start | bytes 98312 | tf_op jit(solution)/shard_map/ppermute | solution.py:227
  23.0 0.0 collective-permute-done.6.far_ref
  23.0 1.3 %outer.1.outer_ref = bf16[32,512,128]{2,1,0:T(8,128)(2,1)S(1)} custom-call(bf16[128,1024]{1,0:T(8,128)(2,1)S(1)} %pad_maximum_fusion.near_ref, bf16[128,1024]{1,0:T(8,128)(2,1)S(1)} %collective-permute-done.6.far_ref, bf16[256,2048]{1,0:T(8,128)(2,1)S(1)} %get-tuple-element.31.scaled_ref), custom_call_target="tpu_custom_call" | custom-call | flops 67108864 | bytes 1048576 | tf_op jit(solution)/shard_map/outer/pallas_call | solution.py:207
  24.3 1.4 %left.1.refs_2_ = f32[64,512]{1,0:T(8,128)S(1)} custom-call(bf16[32,512,128]{2,1,0:T(8,128)(2,1)S(1)} %outer.1.outer_ref, bf16[1024,128]{1,0:T(8,128)(2,1)S(1)} %get-tuple-element.38.owp_ref, bf16[32,64]{1,0:T(8,128)(2,1)S(1)} %get-tuple-element.39.lw_ref), custom_call_target="tpu_custom_call" | custom-call | flops 67108864 | bytes 1048576 | tf_op jit(solution)/shard_map/left/pallas_call | solution.py:207
  25.7 0.0 collective-permute-done.5.refs_0_
  25.7 1.4 %final.1 = f32[512,64]{1,0:T(8,128)} custom-call(f32[16,1024]{1,0:T(8,128)S(1)} %slice.36.keep_ref, bf16[16,1024]{1,0:T(8,128)(2,1)S(1)} %collective-permute-done.5.refs_0_, bf16[32,64]{1,0:T(8,128)(2,1)S(1)} %get-tuple-element.37.refs_1_, f32[64,512]{1,0:T(8,128)S(1)} %left.1.refs_2_, f32[64,512]{1,0:T(8,128)S(1)} %get-tuple-element.40.refs_3_, ...), custom_call_target="tpu_custom_call" | custom-call | bytes 1048576 | tf_op jit(solution)/shard_map/final/pallas_call | solution.py:207
  (10 shorter events, 0.1 us)
Async XLA Ops:
  2.2 6.3 %collective-permute-start = (bf16[16,1024]{1,0:T(8,128)(2,1)S(1)}, bf16[16,1024]{1,0:T(8,128)(2,1)S(1)}, u32[]{:S(2)}, u32[]{:S(2)}) collective-permute-start(bf16[16,1024]{1,0:T(8,128)(2,1)S(1)} %get-tuple-element.30), channel_id=1, source_target_pairs={{0,8},{1,9},{2,10},{3,11},{4,12},{5,13},{6,14},{7,15},{8,0},{9,1},... | collective-permute-start | bytes 98312 | tf_op jit(solution)/shard_map/ppermute | solution.py:227
  8.5 1.6 %collective-permute-start.1 = (bf16[128,1024]{1,0:T(8,128)(2,1)S(1)}, bf16[128,1024]{1,0:T(8,128)(2,1)S(1)}, u32[]{:S(2)}, u32[]{:S(2)}) collective-permute-start(bf16[128,1024]{1,0:T(8,128)(2,1)S(1)} %send.1), channel_id=1, source_target_pairs={{0,1},{1,0},{2,3},{3,2},{4,5},{5,4},{6,7},{7,6},{8,9},{9,8},{10,11... | collective-permute-start | bytes 786440 | tf_op jit(solution)/shard_map/ppermute | solution.py:227
  10.3 5.9 %collective-permute-start.2 = (bf16[64,1024]{1,0:T(8,128)(2,1)S(1)}, bf16[64,1024]{1,0:T(8,128)(2,1)S(1)}, u32[]{:S(2)}, u32[]{:S(2)}) collective-permute-start(bf16[64,1024]{1,0:T(8,128)(2,1)S(1)} %get-tuple-element.48), channel_id=1, source_target_pairs={{0,4},{1,5},{2,6},{3,7},{4,0},{5,1},{6,2},{7,3},{8,12},{9,13},{10,... | collective-permute-start | bytes 393224 | tf_op jit(solution)/shard_map/ppermute | solution.py:227
  11.9 8.1 %collective-permute-start.3 = (bf16[64,1024]{1,0:T(8,128)(2,1)S(1)}, bf16[64,1024]{1,0:T(8,128)(2,1)S(1)}, u32[]{:S(2)}, u32[]{:S(2)}) collective-permute-start(bf16[64,1024]{1,0:T(8,128)(2,1)S(1)} %get-tuple-element.49), channel_id=1, source_target_pairs={{0,2},{1,3},{2,0},{3,1},{4,6},{5,7},{6,4},{7,5},{8,10},{9,11},{10,... | collective-permute-start | bytes 393224 | tf_op jit(solution)/shard_map/ppermute | solution.py:227
  13.4 6.6 %collective-permute-start.4 = (bf16[64,1024]{1,0:T(8,128)(2,1)S(1)}, bf16[64,1024]{1,0:T(8,128)(2,1)S(1)}, u32[]{:S(2)}, u32[]{:S(2)}) collective-permute-start(bf16[64,1024]{1,0:T(8,128)(2,1)S(1)} %get-tuple-element.50), channel_id=1, source_target_pairs={{0,6},{1,7},{2,4},{3,5},{4,2},{5,3},{6,0},{7,1},{8,14},{9,15},{10,... | collective-permute-start | bytes 393224 | tf_op jit(solution)/shard_map/ppermute | solution.py:227
  20.0 3.0 %collective-permute-start.6 = (bf16[128,1024]{1,0:T(8,128)(2,1)S(1)}, bf16[128,1024]{1,0:T(8,128)(2,1)S(1)}, u32[]{:S(2)}, u32[]{:S(2)}) collective-permute-start(bf16[128,1024]{1,0:T(8,128)(2,1)S(1)} %pad_maximum_fusion.near_ref), channel_id=1, source_target_pairs={{0,1},{1,0},{2,3},{3,2},{4,5},{5,4},{6,7},{7,6},{8,9},{9,8},{10,11... | collective-permute-start | bytes 786440 | tf_op jit(solution)/shard_map/ppermute | solution.py:227
  20.1 5.6 %collective-permute-start.5 = (bf16[16,1024]{1,0:T(8,128)(2,1)S(1)}, bf16[16,1024]{1,0:T(8,128)(2,1)S(1)}, u32[]{:S(2)}, u32[]{:S(2)}) collective-permute-start(bf16[16,1024]{1,0:T(8,128)(2,1)S(1)} %split.25), channel_id=1, source_target_pairs={{0,8},{1,9},{2,10},{3,11},{4,12},{5,13},{6,14},{7,15},{8,0},{9,1},... | collective-permute-start | bytes 98312 | tf_op jit(solution)/shard_map/ppermute | solution.py:227

commit v6 on v5

--- a/solution.py
+++ b/solution.py
@@ -17,19 +17,8 @@
     return lax.broadcasted_iota(jnp.int32, shape, axis)
 
 
-def own_presence(mask, me, rows):
-    pick = iota((mask.shape[1], rows), 0) == me * rows + iota((mask.shape[1], rows), 1)
-    return jnp.dot(mask.astype(F32).astype(BF16), pick.astype(F32).astype(BF16), preferred_element_type=F32)
-
-
-def presence_row(own):
-    depth, rows = own.shape
-    count = depth * rows
-    spread = (iota((rows, count), 1) // depth == iota((rows, count), 0)).astype(F32).astype(BF16)
-    wide = jnp.dot(own.astype(BF16), spread, preferred_element_type=F32)
-    return jnp.sum(
-        jnp.where(iota((depth, count), 1) % depth == iota((depth, count), 0), wide, 0.0), axis=0, keepdims=True
-    )
+def bits_of(condition):
+    return condition.astype(F32).astype(BF16)
 
 
 def by_residue(wide_ref, rows):
@@ -40,42 +29,52 @@
 def project_kernel(
     rows,
     x_far, mask_far, res_far, lw_far, rw_far, ow_far, g_far,
-    left_ref, right_ref, x_ref, mask_ref, lw_ref, rw_ref, owp_ref, stack_ref, inverse_ref, g_ref,
-    res_ref, ow_ref, normed, flat, ow_wide, arrived,
+    left_ref, right_ref, x_ref, presence_ref, lw_ref, rw_ref, owp_ref, stack_ref, inverse_ref, g_ref,
+    repeat_ref, diagonal_ref,
+    mask_ref, res_ref, ow_ref, normed, flat, ow_wide, pick, along, arrived,
 ):
     sources = (x_far, mask_far, res_far, lw_far, rw_far, ow_far, g_far)
     targets = (x_ref, mask_ref, res_ref, lw_ref, rw_ref, ow_ref, g_ref)
     copies = [pltpu.make_async_copy(a, b, arrived.at[t]) for t, (a, b) in enumerate(zip(sources, targets))]
     for copy in copies:
         copy.start()
-    for copy in copies[:-1]:
-        copy.wait()
     count, channels = x_ref.shape
     depth, width = mask_ref.shape
     hidden = lw_ref.shape[0]
     pair = ow_ref.shape[1]
     me = lax.axis_index("row")
+    pick[...] = bits_of(iota((width, rows), 0) == me * rows + iota((width, rows), 1))
+    along[...] = bits_of(iota((rows, count), 1) // depth == iota((rows, count), 0))
+    column = iota(repeat_ref.shape, 1)
+    repeat_ref[...] = bits_of((column % depth + depth * (column // 256)) == iota(repeat_ref.shape, 0))
+    diagonal_ref[...] = bits_of(iota((256, 256), 0) // hidden == iota((256, 256), 1) // depth)
+    for copy in copies[:-1]:
+        copy.wait()
     value = x_ref[...].astype(F32)
     centered = value - jnp.mean(value, axis=-1, keepdims=True)
     recip = lax.rsqrt(jnp.mean(centered * centered, axis=-1, keepdims=True) + 1e-05)
     value = centered * recip
     normed[...] = value
-    own = own_presence(mask_ref[...], me, rows)
+    flags = jnp.concatenate(
+        [mask_ref[...].astype(F32), jnp.broadcast_to(res_ref[...].astype(F32), (8, width))], axis=0
+    )
+    own = jnp.dot(flags.astype(BF16), pick[...], preferred_element_type=F32)
+    wide = jnp.dot(own[:depth].astype(BF16), along[...], preferred_element_type=F32)
+    same = iota((depth, count), 1) % depth == iota((depth, count), 0)
+    presence = jnp.sum(jnp.where(same, wide, 0.0), axis=0, keepdims=True)
+    presence_ref[...] = presence
     weights = jnp.concatenate([lw_ref[...], rw_ref[...]], axis=0)
     both = lax.dot_general(weights, by_residue(normed, rows).astype(BF16), NT, preferred_element_type=F32)
-    both = both * presence_row(own)
+    both = both * presence
     left_ref[...] = both[:hidden].astype(BF16)
     for j in range(rows):
         flat[j * hidden : (j + 1) * hidden, :] = both[hidden:, j * depth : (j + 1) * depth]
     right_ref[...] = jnp.concatenate(
         [flat[pl.ds(e, rows, stride=hidden), :] for e in range(hidden)], axis=1
     ).astype(BF16)
-    mask = mask_ref[...].astype(F32)
-    residue = res_ref[...].astype(F32)
-    residue_own = own_presence(jnp.broadcast_to(res_ref[...], (8, width)), me, rows)[:1]
-    tall = jnp.concatenate([mask, jnp.broadcast_to(residue, (8, width))], axis=0).T
-    counts = jnp.dot(tall[:, :depth].astype(BF16), own.astype(BF16), preferred_element_type=F32) + 0.001
-    inverse_ref[...] = tall[:, depth : depth + 1] * residue_own / counts
+    tall = flags.T
+    counts = jnp.dot(tall[:, :depth].astype(BF16), own[:depth].astype(BF16), preferred_element_type=F32) + 0.001
+    inverse_ref[...] = tall[:, depth : depth + 1] * own[depth : depth + 1] / counts
     ow_wide[...] = ow_ref[...].astype(F32)
     for e in range(hidden):
         owp_ref[e * hidden : (e + 1) * hidden, :] = ow_wide[pl.ds(e, hidden, stride=hidden), :].astype(BF16)
@@ -84,7 +83,9 @@
     copies[-1].wait()
 
 
-def spread_kernel(rows, size, g_ref, inverse_ref, left_ref, stack_ref, scaled_ref, spread_ref):
+def spread_kernel(
+    rows, size, g_ref, inverse_ref, left_ref, stack_ref, repeat_ref, diagonal_ref, scaled_ref, spread_ref
+):
     hidden, count = left_ref.shape
     depth = count // rows
     pair = g_ref.shape[2]
@@ -95,14 +96,11 @@
     per = 128 // depth
     blocks = rows // per
     tile = jnp.concatenate([left_ref[:, g * 128 : (g + 1) * 128] for g in range(blocks)], axis=0)
-    column = iota((128, per * 256), 1)
-    repeat = (column % depth + depth * (column // 256)) == iota((128, per * 256), 0)
-    wide = jnp.dot(tile, repeat.astype(F32).astype(BF16), preferred_element_type=F32)
-    diagonal = iota((256, 256), 0) // hidden == iota((256, 256), 1) // depth
+    wide = jnp.dot(tile, repeat_ref[...], preferred_element_type=F32).astype(BF16)
     for i in range(rows):
         g, q = divmod(i, per)
         own_left = wide[g * hidden : (g + 1) * hidden, q * 256 : (q + 1) * 256]
-        block = jnp.where(diagonal, jnp.concatenate([own_left] * fold, axis=0), 0.0).astype(BF16)
+        block = jnp.concatenate([own_left] * fold, axis=0) * diagonal_ref[...]
         out = jnp.dot(stack_ref[...], block, preferred_element_type=F32).astype(BF16)
         for g in range(groups):
             spread_ref[i * pair : (i + 1) * pair, g * 256 : (g + 1) * 256] = out[g * pair : (g + 1) * pair, :]
@@ -121,7 +119,7 @@
 
 
 def keep_kernel(
-    rows, scaled_ref, spread_ref, x_ref, mask_ref, keep_ref, normed_ref, recip_ref, presence_ref, wide
+    rows, scaled_ref, spread_ref, x_ref, keep_ref, normed_ref, recip_ref, wide
 ):
     half = keep_ref.shape[0]
     keep_ref[...] = jnp.dot(scaled_ref[:half, :], spread_ref[...], preferred_element_type=F32)
@@ -131,7 +129,6 @@
     recip = lax.rsqrt(jnp.mean(centered * centered, axis=0, keepdims=True) + 1e-05)
     normed_ref[...] = centered * recip
     recip_ref[...] = recip
-    presence_ref[...] = presence_row(own_presence(mask_ref[...], lax.axis_index("row"), rows))
 
 
 def weigh(weight, value):
@@ -227,28 +224,33 @@
         return lax.ppermute(value, "row", [(d, d ^ bit) for d in range(size)])
 
     sources = (x.reshape(count, channels), mask, residue_mask.reshape(1, width), lw.T, rw.T, ow, g)
-    left, right, x, mask, lw, rw, owp, stack, inverse, g = call(
+    left, right, x, presence, lw, rw, owp, stack, inverse, g, repeat, diagonal = call(
         functools.partial(project_kernel, rows),
         "project",
         (
             near_shape((hidden, count), BF16),
             near_shape((rows, flat_width), BF16),
             near_shape((count, channels), BF16),
-            near_shape(mask.shape, mask.dtype),
+            near_shape((1, count), F32),
             near_shape((hidden, channels), BF16),
             near_shape((hidden, channels), BF16),
             near_shape(ow.shape, BF16),
             near_shape((ow.shape[0] // 256 * pair, 256), BF16),
             near_shape((width, rows), F32),
             near_shape(g.shape, BF16),
+            near_shape((128, 128 // depth * 256), BF16),
+            near_shape((256, 256), BF16),
         ),
         [far(v) for v in sources],
         [
+            pltpu.VMEM(mask.shape, mask.dtype),
             pltpu.VMEM((1, width), residue_mask.dtype),
             pltpu.VMEM(ow.shape, BF16),
             pltpu.VMEM((count, channels), F32),
             pltpu.VMEM((rows * hidden, depth), F32),
             pltpu.VMEM(ow.shape, F32),
+            pltpu.VMEM((width, rows), BF16),
+            pltpu.VMEM((rows, count), BF16),
             pltpu.SemaphoreType.DMA((len(sources),)),
         ],
         in_specs=[pl.BlockSpec(memory_space=pl.ANY)] * len(sources),
@@ -273,7 +275,7 @@
         functools.partial(spread_kernel, rows, size),
         "spread",
         (near_shape((width, rows * pair), BF16), near_shape((rows * pair, flat_width), BF16)),
-        [near(v) for v in (g, inverse, left, stack)],
+        [near(v) for v in (g, inverse, left, stack, repeat, diagonal)],
         flops=2 * 2**30,
     )
     send = call(
@@ -285,16 +287,15 @@
     )
     scaled_again, send, block = lax.optimization_barrier((scaled, send, block))
     got = exchange(send, bits[0])
-    keep, normed, recip, presence = call(
+    keep, normed, recip = call(
         functools.partial(keep_kernel, rows),
         "keep",
         (
             near_shape((width // 2, flat_width), F32),
             near_shape((channels, count), F32),
             near_shape((1, count), F32),
-            near_shape((1, count), F32),
         ),
-        [near(v) for v in (scaled_again, spread, x, mask)],
+        [near(v) for v in (scaled_again, spread, x)],
         [pltpu.VMEM((count, channels), F32)],
         flops=2**30,
     )
@@ -304,11 +305,15 @@
         exchange(jnp.concatenate([piece, block], axis=0), other) for piece, other in zip(sums[1:], partners(stages[0])[1:])
     ]
     cut = sums[0].shape[0]
+    keep = total[:cut]
+    for v in joint[::-1]:
+        keep = lax.optimization_barrier(keep + v[:cut].astype(F32))
+    joint, _ = lax.optimization_barrier((joint, keep))
     near_block = jnp.concatenate([block] + [v[cut:] for v in joint], axis=0)
     far_block = exchange(near_block, bits[0])
-    keep, got = total[:cut], [v[:cut] for v in joint]
+    got = []
     for stage in stages[1:]:
-        total = keep + sum(v.astype(F32) for v in got)
+        total = keep + sum(v.astype(F32) for v in got) if got else keep
         sums = parts(total, stage)
         keep = total[: sums[0].shape[0]]
         got = [exchange(piece, other) for piece, other in zip(sums[1:], partners(stage)[1:])]

time: 27.2 us -> 26.7 us (0.982)
  starting transfers between devices: 10.6 us -> 10.3 us
    ppermute x7, starting transfers between devices: 10.6 us -> 10.3 us  [exchange(): return lax.ppermute(value, 'row', [(d, d ^ bit) for d in range(size)])]
where the time goes in v6:
time: 26.7 us; the launch traced here: 26.6 us
  starting transfers between devices  10.3 us (39%)
  Pallas kernels  9.22 us (35%)
  waiting for transfers between devices  6.74 us (25%)
    ppermute x7, starting transfers between devices, exchange(): return lax.ppermute(value, 'row', [(d, d ^ bit) for d in range(size)])  10.3 us
    pallas_call x7, Pallas kernels, call(): pl.pallas_call(kernel, out_shape=out_shape, in_specs=in_specs or [vmem] *...  9.22 us
    ppermute x7, waiting for transfers between devices, exchange(): return lax.ppermute(value, 'row', [(d, d ^ bit) for d in range(size)])  6.74 us
  transfers between devices with their start and end apart: 7, of which 4 were waited for; matrix products, arithmetic and copies ran while one was open for 0% of the time, Pallas kernels for 19%

profile of v6, /device:TPU:0, one launch (start us, length us, event | category | flops | bytes accessed | tf_op | source)
XLA Modules:
  0.0 26.6 jit_solution(9111921094937599245)
XLA Ops:
  0.0 2.2 %project.1 = (bf16[32,512]{1,0:T(8,128)(2,1)S(1)}, bf16[16,1024]{1,0:T(8,128)(2,1)S(1)}, bf16[512,64]{1,0:T(8,128)(2,1)S(1)}, f32[1,512]{1,0:T(1,128)S(1)}, bf16...) custom-call(bf16[512,64]{1,0:T(8,128)(2,1)} %bitcast.5, ...), custom_call_target="tpu_custom_call" | custom-call | bytes 1048576 | tf_op jit(solution)/shard_map/project/pallas_call | solution.py:204
  2.2 4.1 %collective-permute-start = (bf16[16,1024]{1,0:T(8,128)(2,1)S(1)}, bf16[16,1024]{1,0:T(8,128)(2,1)S(1)}, u32[]{:S(2)}, u32[]{:S(2)}) collective-permute-start(bf16[16,1024]{1,0:T(8,128)(2,1)S(1)} %get-tuple-element.36), channel_id=1, source_target_pairs={{0,8},{1,9},{2,10},{3,11},{4,12},{5,13},{6,14},{7,15},{8,0},{9,1},... | collective-permute-start | bytes 98312 | tf_op jit(solution)/shard_map/ppermute | solution.py:224
  6.3 1.4 %spread.1 = (bf16[256,2048]{1,0:T(8,128)(2,1)S(1)}, bf16[2048,1024]{1,0:T(8,128)(2,1)S(1)}) custom-call(bf16[16,256,128]{2,1,0:T(8,128)(2,1)S(1)} %get-tuple-element.28.g_ref, f32[256,16]{1,0:T(8,128)S(1)} %get-tuple-element.29.inverse_ref, bf16[32,512]{1,0:T(8,128)(2,1)S(1)} %get-tuple-element.30.left_ref, ...), custom_call_target="tpu_custom_call" | custom-call | flops 2147483648 | bytes 1048576 | tf_op jit(solution)/shard_map/spread/pallas_call | solution.py:204
  7.7 0.8 %send.1 = bf16[128,1024]{1,0:T(8,128)(2,1)S(1)} custom-call(bf16[256,2048]{1,0:T(8,128)(2,1)S(1)} %get-tuple-element.37.scaled_ref, bf16[2048,1024]{1,0:T(8,128)(2,1)S(1)} %get-tuple-element.35.spread_ref), custom_call_target="tpu_custom_call" | custom-call | flops 1073741824 | bytes 1048576 | tf_op jit(solution)/shard_map/send/pallas_call | solution.py:204
  8.5 0.0 collective-permute-done
  8.5 0.1 collective-permute-start.1
  8.6 0.8 %keep.1 = (f32[128,1024]{1,0:T(8,128)S(1)}, f32[64,512]{1,0:T(8,128)S(1)}, f32[1,512]{1,0:T(1,128)S(1)}) custom-call(bf16[256,2048]{1,0:T(8,128)(2,1)S(1)} %get-tuple-element.37.scaled_ref, bf16[2048,1024]{1,0:T(8,128)(2,1)S(1)} %get-tuple-element.35.spread_ref, bf16[512,64]{1,0:T(8,128)(2,1)S(1)} %get-tuple-element.38.x_ref), custom_call_target="tpu_custom_call" | custom-call | flops 1073741824 | bytes 1048576 | tf_op jit(solution)/shard_map/keep/pallas_call | solution.py:204
  9.4 0.7 %collective-permute-done.1 = bf16[128,1024]{1,0:T(8,128)(2,1)S(1)} collective-permute-done((bf16[128,1024]{1,0:T(8,128)(2,1)S(1)}, bf16[128,1024]{1,0:T(8,128)(2,1)S(1)}, u32[]{:S(2)}, u32[]{:S(2)}) %collective-permute-start.1) | collective-permute-done | bytes 262176 | tf_op jit(solution)/shard_map/ppermute | solution.py:224
  10.1 0.1 fusion
  10.2 2.6 %collective-permute-start.2 = (bf16[64,1024]{1,0:T(8,128)(2,1)S(1)}, bf16[64,1024]{1,0:T(8,128)(2,1)S(1)}, u32[]{:S(2)}, u32[]{:S(2)}) collective-permute-start(bf16[64,1024]{1,0:T(8,128)(2,1)S(1)} %get-tuple-element.58), channel_id=1, source_target_pairs={{0,6},{1,7},{2,4},{3,5},{4,2},{5,3},{6,0},{7,1},{8,14},{9,15},{10,... | collective-permute-start | bytes 393224 | tf_op jit(solution)/shard_map/ppermute | solution.py:224
  12.8 0.5 %collective-permute-start.3 = (bf16[64,1024]{1,0:T(8,128)(2,1)S(1)}, bf16[64,1024]{1,0:T(8,128)(2,1)S(1)}, u32[]{:S(2)}, u32[]{:S(2)}) collective-permute-start(bf16[64,1024]{1,0:T(8,128)(2,1)S(1)} %get-tuple-element.57), channel_id=1, source_target_pairs={{0,2},{1,3},{2,0},{3,1},{4,6},{5,7},{6,4},{7,5},{8,10},{9,11},{10,... | collective-permute-start | bytes 393224 | tf_op jit(solution)/shard_map/ppermute | solution.py:224
  13.3 0.5 %collective-permute-start.4 = (bf16[64,1024]{1,0:T(8,128)(2,1)S(1)}, bf16[64,1024]{1,0:T(8,128)(2,1)S(1)}, u32[]{:S(2)}, u32[]{:S(2)}) collective-permute-start(bf16[64,1024]{1,0:T(8,128)(2,1)S(1)} %get-tuple-element.56), channel_id=1, source_target_pairs={{0,4},{1,5},{2,6},{3,7},{4,0},{5,1},{6,2},{7,3},{8,12},{9,13},{10,... | collective-permute-start | bytes 393224 | tf_op jit(solution)/shard_map/ppermute | solution.py:224
  13.8 3.2 %collective-permute-done.2 = bf16[64,1024]{1,0:T(8,128)(2,1)S(1)} collective-permute-done((bf16[64,1024]{1,0:T(8,128)(2,1)S(1)}, bf16[64,1024]{1,0:T(8,128)(2,1)S(1)}, u32[]{:S(2)}, u32[]{:S(2)}) %collective-permute-start.2) | collective-permute-done | bytes 131104 | tf_op jit(solution)/shard_map/ppermute | solution.py:224
  17.0 2.6 %collective-permute-done.3 = bf16[64,1024]{1,0:T(8,128)(2,1)S(1)} collective-permute-done((bf16[64,1024]{1,0:T(8,128)(2,1)S(1)}, bf16[64,1024]{1,0:T(8,128)(2,1)S(1)}, u32[]{:S(2)}, u32[]{:S(2)}) %collective-permute-start.3) | collective-permute-done | bytes 131104 | tf_op jit(solution)/shard_map/ppermute | solution.py:224
  19.6 0.2 collective-permute-done.4
  19.9 0.1 collective-permute-start.6
  20.0 2.5 %collective-permute-start.5 = (bf16[16,1024]{1,0:T(8,128)(2,1)S(1)}, bf16[16,1024]{1,0:T(8,128)(2,1)S(1)}, u32[]{:S(2)}, u32[]{:S(2)}) collective-permute-start(bf16[16,1024]{1,0:T(8,128)(2,1)S(1)} %split.25), channel_id=1, source_target_pairs={{0,8},{1,9},{2,10},{3,11},{4,12},{5,13},{6,14},{7,15},{8,0},{9,1},... | collective-permute-start | bytes 98312 | tf_op jit(solution)/shard_map/ppermute | solution.py:224
  22.5 0.0 collective-permute-done.6.far_ref
  22.5 1.3 %outer.1.outer_ref = bf16[32,512,128]{2,1,0:T(8,128)(2,1)S(1)} custom-call(bf16[128,1024]{1,0:T(8,128)(2,1)S(1)} %pad_maximum_fusion.near_ref, bf16[128,1024]{1,0:T(8,128)(2,1)S(1)} %collective-permute-done.6.far_ref, bf16[256,2048]{1,0:T(8,128)(2,1)S(1)} %get-tuple-element.37.scaled_ref), custom_call_target="tpu_custom_call" | custom-call | flops 67108864 | bytes 1048576 | tf_op jit(solution)/shard_map/outer/pallas_call | solution.py:204
  23.8 1.4 %left.1.refs_2_ = f32[64,512]{1,0:T(8,128)S(1)} custom-call(bf16[32,512,128]{2,1,0:T(8,128)(2,1)S(1)} %outer.1.outer_ref, bf16[1024,128]{1,0:T(8,128)(2,1)S(1)} %get-tuple-element.46.owp_ref, bf16[32,64]{1,0:T(8,128)(2,1)S(1)} %get-tuple-element.47.lw_ref), custom_call_target="tpu_custom_call" | custom-call | flops 67108864 | bytes 1048576 | tf_op jit(solution)/shard_map/left/pallas_call | solution.py:204
  25.2 0.0 collective-permute-done.5.refs_0_
  25.2 1.4 %final.1 = f32[512,64]{1,0:T(8,128)} custom-call(f32[16,1024]{1,0:T(8,128)S(1)} %slice.36.keep_ref, bf16[16,1024]{1,0:T(8,128)(2,1)S(1)} %collective-permute-done.5.refs_0_, bf16[32,64]{1,0:T(8,128)(2,1)S(1)} %get-tuple-element.42.refs_1_, f32[64,512]{1,0:T(8,128)S(1)} %left.1.refs_2_, f32[64,512]{1,0:T(8,128)S(1)} %get-tuple-element.48.refs_3_, ...), custom_call_target="tpu_custom_call" | custom-call | bytes 1048576 | tf_op jit(solution)/shard_map/final/pallas_call | solution.py:204
  (12 shorter events, 0.1 us)
Async XLA Ops:
  2.2 6.3 %collective-permute-start = (bf16[16,1024]{1,0:T(8,128)(2,1)S(1)}, bf16[16,1024]{1,0:T(8,128)(2,1)S(1)}, u32[]{:S(2)}, u32[]{:S(2)}) collective-permute-start(bf16[16,1024]{1,0:T(8,128)(2,1)S(1)} %get-tuple-element.36), channel_id=1, source_target_pairs={{0,8},{1,9},{2,10},{3,11},{4,12},{5,13},{6,14},{7,15},{8,0},{9,1},... | collective-permute-start | bytes 98312 | tf_op jit(solution)/shard_map/ppermute | solution.py:224
  8.5 1.6 %collective-permute-start.1 = (bf16[128,1024]{1,0:T(8,128)(2,1)S(1)}, bf16[128,1024]{1,0:T(8,128)(2,1)S(1)}, u32[]{:S(2)}, u32[]{:S(2)}) collective-permute-start(bf16[128,1024]{1,0:T(8,128)(2,1)S(1)} %send.1), channel_id=1, source_target_pairs={{0,1},{1,0},{2,3},{3,2},{4,5},{5,4},{6,7},{7,6},{8,9},{9,8},{10,11... | collective-permute-start | bytes 786440 | tf_op jit(solution)/shard_map/ppermute | solution.py:224
  10.2 6.7 %collective-permute-start.2 = (bf16[64,1024]{1,0:T(8,128)(2,1)S(1)}, bf16[64,1024]{1,0:T(8,128)(2,1)S(1)}, u32[]{:S(2)}, u32[]{:S(2)}) collective-permute-start(bf16[64,1024]{1,0:T(8,128)(2,1)S(1)} %get-tuple-element.58), channel_id=1, source_target_pairs={{0,6},{1,7},{2,4},{3,5},{4,2},{5,3},{6,0},{7,1},{8,14},{9,15},{10,... | collective-permute-start | bytes 393224 | tf_op jit(solution)/shard_map/ppermute | solution.py:224
  12.8 6.7 %collective-permute-start.3 = (bf16[64,1024]{1,0:T(8,128)(2,1)S(1)}, bf16[64,1024]{1,0:T(8,128)(2,1)S(1)}, u32[]{:S(2)}, u32[]{:S(2)}) collective-permute-start(bf16[64,1024]{1,0:T(8,128)(2,1)S(1)} %get-tuple-element.57), channel_id=1, source_target_pairs={{0,2},{1,3},{2,0},{3,1},{4,6},{5,7},{6,4},{7,5},{8,10},{9,11},{10,... | collective-permute-start | bytes 393224 | tf_op jit(solution)/shard_map/ppermute | solution.py:224
  13.3 6.5 %collective-permute-start.4 = (bf16[64,1024]{1,0:T(8,128)(2,1)S(1)}, bf16[64,1024]{1,0:T(8,128)(2,1)S(1)}, u32[]{:S(2)}, u32[]{:S(2)}) collective-permute-start(bf16[64,1024]{1,0:T(8,128)(2,1)S(1)} %get-tuple-element.56), channel_id=1, source_target_pairs={{0,4},{1,5},{2,6},{3,7},{4,0},{5,1},{6,2},{7,3},{8,12},{9,13},{10,... | collective-permute-start | bytes 393224 | tf_op jit(solution)/shard_map/ppermute | solution.py:224
  19.9 2.6 %collective-permute-start.6 = (bf16[128,1024]{1,0:T(8,128)(2,1)S(1)}, bf16[128,1024]{1,0:T(8,128)(2,1)S(1)}, u32[]{:S(2)}, u32[]{:S(2)}) collective-permute-start(bf16[128,1024]{1,0:T(8,128)(2,1)S(1)} %pad_maximum_fusion.near_ref), channel_id=1, source_target_pairs={{0,1},{1,0},{2,3},{3,2},{4,5},{5,4},{6,7},{7,6},{8,9},{9,8},{10,11... | collective-permute-start | bytes 786440 | tf_op jit(solution)/shard_map/ppermute | solution.py:224
  20.0 5.2 %collective-permute-start.5 = (bf16[16,1024]{1,0:T(8,128)(2,1)S(1)}, bf16[16,1024]{1,0:T(8,128)(2,1)S(1)}, u32[]{:S(2)}, u32[]{:S(2)}) collective-permute-start(bf16[16,1024]{1,0:T(8,128)(2,1)S(1)} %split.25), channel_id=1, source_target_pairs={{0,8},{1,9},{2,10},{3,11},{4,12},{5,13},{6,14},{7,15},{8,0},{9,1},... | collective-permute-start | bytes 98312 | tf_op jit(solution)/shard_map/ppermute | solution.py:224

commit v7 on v6

--- a/solution.py
+++ b/solution.py
@@ -168,7 +168,7 @@
 
 
 def final_kernel(rows, keep_ref, *refs):
-    *got_refs, rw_ref, grad_ref, normed_ref, recip_ref, presence_ref, out_ref, flat = refs
+    *got_refs, rw_ref, grad_ref, normed_ref, recip_ref, presence_ref, out_far, flat, staged, sent = refs
     hidden = rw_ref.shape[0]
     depth = keep_ref.shape[1] // hidden
     total = keep_ref[...]
@@ -176,14 +176,26 @@
         total = total + got_ref[...].astype(F32)
     for e in range(hidden):
         flat[pl.ds(e, rows, stride=hidden), :] = total[:, e * depth : (e + 1) * depth]
-    right = jnp.concatenate([flat[j * hidden : (j + 1) * hidden, :] for j in range(rows)], axis=1)
-    grad = (weigh(rw_ref[...], right) + grad_ref[...]) * presence_ref[...]
-    normed = normed_ref[...]
-    mean = jnp.mean(grad, axis=0, keepdims=True)
-    cross = jnp.mean(grad * normed, axis=0, keepdims=True)
-    out = (recip_ref[...] * (grad - mean - normed * cross)).T
-    for i in range(rows):
-        out_ref[pl.ds(i, depth, stride=rows), :] = out[i * depth : (i + 1) * depth, :]
+    part = rows // 2
+    copies = []
+    for h in range(2):
+        lanes = slice(h * part * depth, (h + 1) * part * depth)
+        right = jnp.concatenate(
+            [flat[j * hidden : (j + 1) * hidden, :] for j in range(h * part, (h + 1) * part)], axis=1
+        )
+        grad = (weigh(rw_ref[...], right) + grad_ref[:, lanes]) * presence_ref[:, lanes]
+        normed = normed_ref[:, lanes]
+        mean = jnp.mean(grad, axis=0, keepdims=True)
+        cross = jnp.mean(grad * normed, axis=0, keepdims=True)
+        out = (recip_ref[:, lanes] * (grad - mean - normed * cross)).T
+        for i in range(part):
+            staged[h, :, i, :] = out[i * depth : (i + 1) * depth, :]
+        copies.append(
+            pltpu.make_async_copy(staged.at[h], out_far.at[:, h * part : (h + 1) * part, :], sent.at[h])
+        )
+        copies[-1].start()
+    for copy in copies:
+        copy.wait()
 
 
 def near_shape(dims, dtype):
@@ -198,9 +210,9 @@
     return pltpu.with_memory_space_constraint(value, pltpu.HBM)
 
 
-def call(kernel, name, out_shape, args, scratch=(), flops=0, in_specs=None):
+def call(kernel, name, out_shape, args, scratch=(), flops=0, in_specs=None, out_specs=None):
     vmem = pl.BlockSpec(memory_space=pltpu.VMEM)
-    out_specs = (vmem,) * len(out_shape) if isinstance(out_shape, tuple) else vmem
+    out_specs = out_specs or ((vmem,) * len(out_shape) if isinstance(out_shape, tuple) else vmem)
     return pl.pallas_call(
         kernel,
         out_shape=out_shape,
@@ -335,11 +347,16 @@
     out = call(
         functools.partial(final_kernel, rows),
         "final",
-        jax.ShapeDtypeStruct((count, channels), F32),
+        jax.ShapeDtypeStruct((depth, rows, channels), F32),
         [near(v) for v in (keep, *got, rw, grad, normed, recip, presence)],
-        [pltpu.VMEM((rows * hidden, depth), F32)],
-    )
-    return out.reshape(depth, rows, channels)
+        [
+            pltpu.VMEM((rows * hidden, depth), F32),
+            pltpu.VMEM((2, depth, rows // 2, channels), F32),
+            pltpu.SemaphoreType.DMA((2,)),
+        ],
+        out_specs=pl.BlockSpec(memory_space=pl.ANY),
+    )
+    return out
 
 
 def solution(mesh):

time: 26.7 us -> 26.7 us (level)
  no operation moved by 1% of the time
where the time goes in v7:
time: 26.7 us; the launch traced here: 26.6 us
  starting transfers between devices  10.3 us (39%)
  Pallas kernels  9.2 us (34%)
  waiting for transfers between devices  6.74 us (25%)
    ppermute x7, starting transfers between devices, exchange(): return lax.ppermute(value, 'row', [(d, d ^ bit) for d in range(size)])  10.3 us
    pallas_call x7, Pallas kernels, call(): pl.pallas_call(kernel, out_shape=out_shape, in_specs=in_specs or [vmem] *...  9.2 us
    ppermute x7, waiting for transfers between devices, exchange(): return lax.ppermute(value, 'row', [(d, d ^ bit) for d in range(size)])  6.74 us
  transfers between devices with their start and end apart: 7, of which 4 were waited for; matrix products, arithmetic and copies ran while one was open for 0% of the time, Pallas kernels for 19%

profile of v7, /device:TPU:0, one launch (start us, length us, event | category | flops | bytes accessed | tf_op | source)
XLA Modules:
  0.0 26.6 jit_solution(11138280485277891056)
XLA Ops:
  0.0 2.2 %project.1 = (bf16[32,512]{1,0:T(8,128)(2,1)S(1)}, bf16[16,1024]{1,0:T(8,128)(2,1)S(1)}, bf16[512,64]{1,0:T(8,128)(2,1)S(1)}, f32[1,512]{1,0:T(1,128)S(1)}, bf16...) custom-call(bf16[512,64]{1,0:T(8,128)(2,1)} %bitcast.4, ...), custom_call_target="tpu_custom_call" | custom-call | bytes 1048576 | tf_op jit(solution)/shard_map/project/pallas_call | solution.py:216
  2.2 4.1 %collective-permute-start = (bf16[16,1024]{1,0:T(8,128)(2,1)S(1)}, bf16[16,1024]{1,0:T(8,128)(2,1)S(1)}, u32[]{:S(2)}, u32[]{:S(2)}) collective-permute-start(bf16[16,1024]{1,0:T(8,128)(2,1)S(1)} %get-tuple-element.36), channel_id=1, source_target_pairs={{0,8},{1,9},{2,10},{3,11},{4,12},{5,13},{6,14},{7,15},{8,0},{9,1},... | collective-permute-start | bytes 98312 | tf_op jit(solution)/shard_map/ppermute | solution.py:236
  6.3 1.4 %spread.1 = (bf16[256,2048]{1,0:T(8,128)(2,1)S(1)}, bf16[2048,1024]{1,0:T(8,128)(2,1)S(1)}) custom-call(bf16[16,256,128]{2,1,0:T(8,128)(2,1)S(1)} %get-tuple-element.28.g_ref, f32[256,16]{1,0:T(8,128)S(1)} %get-tuple-element.29.inverse_ref, bf16[32,512]{1,0:T(8,128)(2,1)S(1)} %get-tuple-element.30.left_ref, ...), custom_call_target="tpu_custom_call" | custom-call | flops 2147483648 | bytes 1048576 | tf_op jit(solution)/shard_map/spread/pallas_call | solution.py:216
  7.7 0.8 %send.1 = bf16[128,1024]{1,0:T(8,128)(2,1)S(1)} custom-call(bf16[256,2048]{1,0:T(8,128)(2,1)S(1)} %get-tuple-element.37.scaled_ref, bf16[2048,1024]{1,0:T(8,128)(2,1)S(1)} %get-tuple-element.35.spread_ref), custom_call_target="tpu_custom_call" | custom-call | flops 1073741824 | bytes 1048576 | tf_op jit(solution)/shard_map/send/pallas_call | solution.py:216
  8.5 0.0 collective-permute-done
  8.5 0.1 collective-permute-start.1
  8.6 0.8 %keep.1 = (f32[128,1024]{1,0:T(8,128)S(1)}, f32[64,512]{1,0:T(8,128)S(1)}, f32[1,512]{1,0:T(1,128)S(1)}) custom-call(bf16[256,2048]{1,0:T(8,128)(2,1)S(1)} %get-tuple-element.37.scaled_ref, bf16[2048,1024]{1,0:T(8,128)(2,1)S(1)} %get-tuple-element.35.spread_ref, bf16[512,64]{1,0:T(8,128)(2,1)S(1)} %get-tuple-element.38.x_ref), custom_call_target="tpu_custom_call" | custom-call | flops 1073741824 | bytes 1048576 | tf_op jit(solution)/shard_map/keep/pallas_call | solution.py:216
  9.4 0.7 %collective-permute-done.1 = bf16[128,1024]{1,0:T(8,128)(2,1)S(1)} collective-permute-done((bf16[128,1024]{1,0:T(8,128)(2,1)S(1)}, bf16[128,1024]{1,0:T(8,128)(2,1)S(1)}, u32[]{:S(2)}, u32[]{:S(2)}) %collective-permute-start.1) | collective-permute-done | bytes 262176 | tf_op jit(solution)/shard_map/ppermute | solution.py:236
  10.1 0.1 fusion
  10.2 2.6 %collective-permute-start.2 = (bf16[64,1024]{1,0:T(8,128)(2,1)S(1)}, bf16[64,1024]{1,0:T(8,128)(2,1)S(1)}, u32[]{:S(2)}, u32[]{:S(2)}) collective-permute-start(bf16[64,1024]{1,0:T(8,128)(2,1)S(1)} %get-tuple-element.58), channel_id=1, source_target_pairs={{0,6},{1,7},{2,4},{3,5},{4,2},{5,3},{6,0},{7,1},{8,14},{9,15},{10,... | collective-permute-start | bytes 393224 | tf_op jit(solution)/shard_map/ppermute | solution.py:236
  12.8 0.5 %collective-permute-start.3 = (bf16[64,1024]{1,0:T(8,128)(2,1)S(1)}, bf16[64,1024]{1,0:T(8,128)(2,1)S(1)}, u32[]{:S(2)}, u32[]{:S(2)}) collective-permute-start(bf16[64,1024]{1,0:T(8,128)(2,1)S(1)} %get-tuple-element.57), channel_id=1, source_target_pairs={{0,2},{1,3},{2,0},{3,1},{4,6},{5,7},{6,4},{7,5},{8,10},{9,11},{10,... | collective-permute-start | bytes 393224 | tf_op jit(solution)/shard_map/ppermute | solution.py:236
  13.3 0.5 %collective-permute-start.4 = (bf16[64,1024]{1,0:T(8,128)(2,1)S(1)}, bf16[64,1024]{1,0:T(8,128)(2,1)S(1)}, u32[]{:S(2)}, u32[]{:S(2)}) collective-permute-start(bf16[64,1024]{1,0:T(8,128)(2,1)S(1)} %get-tuple-element.56), channel_id=1, source_target_pairs={{0,4},{1,5},{2,6},{3,7},{4,0},{5,1},{6,2},{7,3},{8,12},{9,13},{10,... | collective-permute-start | bytes 393224 | tf_op jit(solution)/shard_map/ppermute | solution.py:236
  13.8 3.2 %collective-permute-done.2 = bf16[64,1024]{1,0:T(8,128)(2,1)S(1)} collective-permute-done((bf16[64,1024]{1,0:T(8,128)(2,1)S(1)}, bf16[64,1024]{1,0:T(8,128)(2,1)S(1)}, u32[]{:S(2)}, u32[]{:S(2)}) %collective-permute-start.2) | collective-permute-done | bytes 131104 | tf_op jit(solution)/shard_map/ppermute | solution.py:236
  17.0 2.6 %collective-permute-done.3 = bf16[64,1024]{1,0:T(8,128)(2,1)S(1)} collective-permute-done((bf16[64,1024]{1,0:T(8,128)(2,1)S(1)}, bf16[64,1024]{1,0:T(8,128)(2,1)S(1)}, u32[]{:S(2)}, u32[]{:S(2)}) %collective-permute-start.3) | collective-permute-done | bytes 131104 | tf_op jit(solution)/shard_map/ppermute | solution.py:236
  19.6 0.2 collective-permute-done.4
  19.9 0.1 collective-permute-start.6
  20.0 2.5 %collective-permute-start.5 = (bf16[16,1024]{1,0:T(8,128)(2,1)S(1)}, bf16[16,1024]{1,0:T(8,128)(2,1)S(1)}, u32[]{:S(2)}, u32[]{:S(2)}) collective-permute-start(bf16[16,1024]{1,0:T(8,128)(2,1)S(1)} %split.25), channel_id=1, source_target_pairs={{0,8},{1,9},{2,10},{3,11},{4,12},{5,13},{6,14},{7,15},{8,0},{9,1},... | collective-permute-start | bytes 98312 | tf_op jit(solution)/shard_map/ppermute | solution.py:236
  22.5 0.0 collective-permute-done.6.far_ref
  22.5 1.3 %outer.1.outer_ref = bf16[32,512,128]{2,1,0:T(8,128)(2,1)S(1)} custom-call(bf16[128,1024]{1,0:T(8,128)(2,1)S(1)} %pad_maximum_fusion.near_ref, bf16[128,1024]{1,0:T(8,128)(2,1)S(1)} %collective-permute-done.6.far_ref, bf16[256,2048]{1,0:T(8,128)(2,1)S(1)} %get-tuple-element.37.scaled_ref), custom_call_target="tpu_custom_call" | custom-call | flops 67108864 | bytes 1048576 | tf_op jit(solution)/shard_map/outer/pallas_call | solution.py:216
  23.8 1.4 %left.1.refs_2_ = f32[64,512]{1,0:T(8,128)S(1)} custom-call(bf16[32,512,128]{2,1,0:T(8,128)(2,1)S(1)} %outer.1.outer_ref, bf16[1024,128]{1,0:T(8,128)(2,1)S(1)} %get-tuple-element.46.owp_ref, bf16[32,64]{1,0:T(8,128)(2,1)S(1)} %get-tuple-element.47.lw_ref), custom_call_target="tpu_custom_call" | custom-call | flops 67108864 | bytes 1048576 | tf_op jit(solution)/shard_map/left/pallas_call | solution.py:216
  25.2 0.0 collective-permute-done.5.refs_0_
  25.2 1.3 %final.1 = f32[32,16,64]{2,1,0:T(8,128)} custom-call(f32[16,1024]{1,0:T(8,128)S(1)} %slice.36.keep_ref, bf16[16,1024]{1,0:T(8,128)(2,1)S(1)} %collective-permute-done.5.refs_0_, bf16[32,64]{1,0:T(8,128)(2,1)S(1)} %get-tuple-element.42.refs_1_, f32[64,512]{1,0:T(8,128)S(1)} %left.1.refs_2_, f32[64,512]{1,0:T(8,128)S(1)} %get-tuple-element.48.refs_3_, ...), custom_call_target="tpu_custom_call" | custom-call | bytes 1048576 | tf_op jit(solution)/shard_map/final/pallas_call | solution.py:216
  (12 shorter events, 0.1 us)
Async XLA Ops:
  2.2 6.3 %collective-permute-start = (bf16[16,1024]{1,0:T(8,128)(2,1)S(1)}, bf16[16,1024]{1,0:T(8,128)(2,1)S(1)}, u32[]{:S(2)}, u32[]{:S(2)}) collective-permute-start(bf16[16,1024]{1,0:T(8,128)(2,1)S(1)} %get-tuple-element.36), channel_id=1, source_target_pairs={{0,8},{1,9},{2,10},{3,11},{4,12},{5,13},{6,14},{7,15},{8,0},{9,1},... | collective-permute-start | bytes 98312 | tf_op jit(solution)/shard_map/ppermute | solution.py:236
  8.5 1.6 %collective-permute-start.1 = (bf16[128,1024]{1,0:T(8,128)(2,1)S(1)}, bf16[128,1024]{1,0:T(8,128)(2,1)S(1)}, u32[]{:S(2)}, u32[]{:S(2)}) collective-permute-start(bf16[128,1024]{1,0:T(8,128)(2,1)S(1)} %send.1), channel_id=1, source_target_pairs={{0,1},{1,0},{2,3},{3,2},{4,5},{5,4},{6,7},{7,6},{8,9},{9,8},{10,11... | collective-permute-start | bytes 786440 | tf_op jit(solution)/shard_map/ppermute | solution.py:236
  10.2 6.7 %collective-permute-start.2 = (bf16[64,1024]{1,0:T(8,128)(2,1)S(1)}, bf16[64,1024]{1,0:T(8,128)(2,1)S(1)}, u32[]{:S(2)}, u32[]{:S(2)}) collective-permute-start(bf16[64,1024]{1,0:T(8,128)(2,1)S(1)} %get-tuple-element.58), channel_id=1, source_target_pairs={{0,6},{1,7},{2,4},{3,5},{4,2},{5,3},{6,0},{7,1},{8,14},{9,15},{10,... | collective-permute-start | bytes 393224 | tf_op jit(solution)/shard_map/ppermute | solution.py:236
  12.8 6.7 %collective-permute-start.3 = (bf16[64,1024]{1,0:T(8,128)(2,1)S(1)}, bf16[64,1024]{1,0:T(8,128)(2,1)S(1)}, u32[]{:S(2)}, u32[]{:S(2)}) collective-permute-start(bf16[64,1024]{1,0:T(8,128)(2,1)S(1)} %get-tuple-element.57), channel_id=1, source_target_pairs={{0,2},{1,3},{2,0},{3,1},{4,6},{5,7},{6,4},{7,5},{8,10},{9,11},{10,... | collective-permute-start | bytes 393224 | tf_op jit(solution)/shard_map/ppermute | solution.py:236
  13.3 6.5 %collective-permute-start.4 = (bf16[64,1024]{1,0:T(8,128)(2,1)S(1)}, bf16[64,1024]{1,0:T(8,128)(2,1)S(1)}, u32[]{:S(2)}, u32[]{:S(2)}) collective-permute-start(bf16[64,1024]{1,0:T(8,128)(2,1)S(1)} %get-tuple-element.56), channel_id=1, source_target_pairs={{0,4},{1,5},{2,6},{3,7},{4,0},{5,1},{6,2},{7,3},{8,12},{9,13},{10,... | collective-permute-start | bytes 393224 | tf_op jit(solution)/shard_map/ppermute | solution.py:236
  19.9 2.6 %collective-permute-start.6 = (bf16[128,1024]{1,0:T(8,128)(2,1)S(1)}, bf16[128,1024]{1,0:T(8,128)(2,1)S(1)}, u32[]{:S(2)}, u32[]{:S(2)}) collective-permute-start(bf16[128,1024]{1,0:T(8,128)(2,1)S(1)} %pad_maximum_fusion.near_ref), channel_id=1, source_target_pairs={{0,1},{1,0},{2,3},{3,2},{4,5},{5,4},{6,7},{7,6},{8,9},{9,8},{10,11... | collective-permute-start | bytes 786440 | tf_op jit(solution)/shard_map/ppermute | solution.py:236
  20.0 5.2 %collective-permute-start.5 = (bf16[16,1024]{1,0:T(8,128)(2,1)S(1)}, bf16[16,1024]{1,0:T(8,128)(2,1)S(1)}, u32[]{:S(2)}, u32[]{:S(2)}) collective-permute-start(bf16[16,1024]{1,0:T(8,128)(2,1)S(1)} %split.25), channel_id=1, source_target_pairs={{0,8},{1,9},{2,10},{3,11},{4,12},{5,13},{6,14},{7,15},{8,0},{9,1},... | collective-permute-start | bytes 98312 | tf_op jit(solution)/shard_map/ppermute | solution.py:236
